TPU v7x, 32 devices: a whole 2x2x4 slice. The times are simulated.
32 devices in a mesh: seq: 16 (over z, y, x), chan: 2 (over core).
Axes of the slice: x: 2, y: 2, z: 4, core: 2. Of those that a mesh axis runs over, the one named last changes fastest.
Arguments:
- streams: bfloat16 [3, 4096, 8192], P(None, 'seq', 'chan'), may hold values from -6 to 6
- short_filter: float32 [3, 3, 8192], P(None, None, 'chan'), may hold values from -3 to 3
- pole_rates: float32 [16, 8192], P(None, 'chan'), may hold values from 2.4414063e-05 to 0.03
- residues: float32 [16, 8192], P(None, 'chan'), may hold values from -3 to 3
- direct: float32 [8192], P('chan'), may hold values from -3 to 3
- doc_lengths: int32 [4], replicated, may hold values from 1 to 2048, 4096 in all
- targets: int32 [4096], P('seq'), may hold values from 0 to 511
- unembed: bfloat16 [8192, 512], P('chan'), may hold values from -0.7 to 0.7
Outputs:
- gated_out: bfloat16 [4096, 8192], P('seq', 'chan')
- token_loss: float32 [4096], P('seq')
All inputs are finite; a program needn't handle non-finite values.
Results may differ from a plain program's by a relative error of at most 0.012.
Values may be sent and summed in bfloat16 or wider, within the bound.
A program may use at most 128 MiB of HBM per device.

v0:
```python
import jax
import jax.numpy as jnp
from jax import lax
from jax.sharding import PartitionSpec as P


def shifted(block, axis, distance):
    devices = range(lax.axis_size(axis))
    route = [(i - distance, i) for i in devices if i - distance in devices]
    return lax.ppermute(block, axis, route)


def local(streams, short_filter, pole_rates, residues, direct, doc_lengths, targets, unembed):
    block_len = streams.shape[1]
    chans = streams.shape[2]
    pole_count = pole_rates.shape[0]
    group_size = 4
    group_count = pole_count // group_size
    block_id = lax.axis_index("seq")
    first_pos = block_id * block_len
    local_ids = jnp.arange(block_len, dtype=jnp.int32)
    local_float = local_ids.astype(jnp.float32)
    position = first_pos + local_ids
    doc_first = jnp.cumsum(doc_lengths) - doc_lengths
    chosen = jnp.where(doc_first[None, :] <= position[:, None], doc_first[None, :], 0)
    doc_start = jnp.max(chosen, axis=1)
    edge_rows = shifted(streams[:, block_len - 2 :, :], "seq", 1)
    extended = jnp.concatenate([edge_rows, streams], axis=1).astype(jnp.float32)
    filtered = short_filter[:, 0, None, :] * extended[:, 2:, :]
    for shift_by in range(1, 3):
        in_doc = (position - shift_by >= doc_start).astype(jnp.float32)
        window_rows = extended[:, 2 - shift_by : 2 - shift_by + block_len, :]
        filtered = (
            filtered + short_filter[:, shift_by, None, :] * window_rows * in_doc[None, :, None]
        )
    q_stream = filtered[0]
    driver = filtered[1] * filtered[2]
    rel_start = doc_start - first_pos
    same_doc = (
        (local_ids[None, :] <= local_ids[:, None]) & (local_ids[None, :] >= rel_start[:, None])
    ).astype(jnp.float32)
    rate_groups = pole_rates.reshape(group_count, group_size, chans)
    residue_groups = residues.reshape(group_count, group_size, chans)

    def block_states(members):
        rate_g, residue_g = members
        rising = jnp.exp(rate_g[:, None, :] * local_float[None, :, None])
        weighted = rising * (1.0 - jnp.exp(-rate_g))[:, None, :] * driver[None, :, :]
        summed = jnp.einsum("ts,psc->ptc", same_doc, weighted, precision=lax.Precision.HIGHEST)
        states_g = summed * jnp.exp(-rate_g[:, None, :] * local_float[None, :, None])
        return (jnp.sum(residue_g[:, None, :] * states_g, axis=0), states_g[:, block_len - 1, :])

    partial_out, end_groups = lax.map(block_states, (rate_groups, residue_groups))
    long_out = jnp.sum(partial_out, axis=0)
    end_states = end_groups.reshape(pole_count, chans)
    keep_block = (doc_start[block_len - 1] < first_pos).astype(jnp.float32)
    transfer = jnp.exp(-pole_rates * block_len) * keep_block

    def relay_step(turn, arriving):
        return shifted(transfer * arriving + end_states, "seq", 1)

    incoming = lax.fori_loop(0, lax.axis_size("seq") - 1, relay_step, jnp.zeros_like(end_states))
    carried_in = (doc_start < first_pos).astype(jnp.float32)
    incoming_groups = incoming.reshape(group_count, group_size, chans)
    for group_id in range(group_count):
        weight_in = residue_groups[group_id] * incoming_groups[group_id]
        fading = jnp.exp(-rate_groups[group_id][:, None, :] * (local_float + 1.0)[None, :, None])
        long_out = long_out + carried_in[:, None] * jnp.sum(weight_in[:, None, :] * fading, axis=0)
    gated_out = (q_stream * (long_out + direct[None, :] * driver)).astype(jnp.bfloat16)
    partial_logits = jnp.dot(gated_out, unembed, preferred_element_type=jnp.float32)
    vocab_size = unembed.shape[1]
    logits = lax.psum(partial_logits.astype(jnp.bfloat16), "chan").astype(jnp.float32)
    peak = jnp.max(logits, axis=1)
    exp_total = jnp.sum(jnp.exp(logits - peak[:, None]), axis=1)
    vocab_ids = jnp.arange(vocab_size, dtype=jnp.int32)
    picked = jnp.sum(jnp.where(targets[:, None] == vocab_ids[None, :], logits, 0.0), axis=1)
    token_loss = peak + jnp.log(exp_total) - picked
    return (gated_out, token_loss)


def solution(mesh):
    in_specs = (
        P(None, "seq", "chan"),
        P(None, None, "chan"),
        P(None, "chan"),
        P(None, "chan"),
        P("chan"),
        P(),
        P("seq"),
        P("chan", None),
    )
    out_specs = (P("seq", "chan"), P("seq"))
    return jax.shard_map(local, mesh=mesh, in_specs=in_specs, out_specs=out_specs, check_vma=False)
```

profile of v0, /device:TPU:29, one launch (start us, length us, event | category | flops | bytes accessed | tf_op | source)
XLA Modules:
  0.0 409.6 jit_solution(805786969152960831)
XLA Ops:
  8.2 3.1 collective-permute-start.1
  20.6 4.7 %maximum_convert_fusion = f32[3,258,4096]{2,1,0:T(8,128)S(1)} fusion(bf16[3,256,4096]{2,1,0:T(8,128)(2,1)} %param.12, bf16[3,2,4096]{2,1,0:T(2,128)(2,1)S(1)} %collective-permute-done.1), kind=kLoop, calls=%fused_computation.38 | loop fusion | flops 12681216 | bytes 19021824 | tf_op jit(solution)/shard_map/convert_element_type | solution.py:28
  25.3 7.3 %fusion.21 = f32[3,256,4096]{2,1,0:T(8,128)} fusion(f32[3,258,4096]{2,1,0:T(8,128)S(1)} %maximum_convert_fusion, f32[256]{0:T(256)S(1)} %get-tuple-element.155, f32[3,4096]{1,0:T(4,128)S(1)} %get-tuple-element.157, f32[256]{0:T(256)S(1)} %get-tuple-element.156, f32[3,4096]{1,0:T(4,128)S(1)} %get-tuple-element.158, f32[3,4096]{1,0:T(4,128)S(1)} %bitcast.47), kind=kLoop, calls=%fused_computation.33 | loop fusion | flops 22020096 | bytes 50481152 | tf_op jit(solution)/shard_map/add | solution.py:34
  32.6 6.1 %fusion.24 = f32[256,4096]{1,0:T(8,128)} fusion(f32[3,256,4096]{2,1,0:T(8,128)} %fusion.21), kind=kLoop, calls=%fused_computation.40 | loop fusion | flops 1048576 | bytes 12582912 | tf_op jit(solution)/shard_map/mul | solution.py:37
  38.7 140.2 %while.25 = (s32[]{:T(128)}, f32[4,256,4096]{2,1,0:T(8,128)}, f32[4,4,4096]{2,1,0:T(4,128)S(1)}, f32[4,4,4096]{2,1,0:T(4,128)S(1)}, f32[4,4,4096]{2,1,0:T(4,128)...) while((s32[]{:T(128)}, f32[4,256,4096]{2,1,0:T(8,128)}, ...), condition=%wide.region_4.5_spmd.clone.clone, body=%wide.region_2.4_spmd.clone.clone.sunk | while | flops 12913524736 | bytes 34540652 | solution.py:53
  38.8 32.6 %multiply_reduce_fusion.6 = (f32[256,4096]{1,0:T(8,128)S(1)}, f32[4,256,4096]{2,1,0:T(8,128)S(1)}) fusion(f32[4,4096]{1,0:T(4,128)S(1)} %dynamic-slice_bitcast_fusion.4, f32[256]{0:T(256)S(1)} %iota_convert_fusion.2, f32[4,4096]{1,0:T(4,128)S(1)} %neg.47, s32[256]{0:T(256)S(1)} %get-tuple-element.257, f32[256,4096]{1,0:T(8,128)} %get-tuple-element.256, ...), kind=kOutput, calls=%fused_computation.4.clone.1 | convolution fusion | flops 12913475584 | bytes 25430016 | tf_op jit(solution)/shard_map/while/body/eval_jaxpr/ts,psc->ptc/dot_general | solution.py:49
  73.8 32.6 %multiply_reduce_fusion.6 = (f32[256,4096]{1,0:T(8,128)S(1)}, f32[4,256,4096]{2,1,0:T(8,128)S(1)}) fusion(f32[4,4096]{1,0:T(4,128)S(1)} %dynamic-slice_bitcast_fusion.4, f32[256]{0:T(256)S(1)} %iota_convert_fusion.2, f32[4,4096]{1,0:T(4,128)S(1)} %neg.47, s32[256]{0:T(256)S(1)} %get-tuple-element.257, f32[256,4096]{1,0:T(8,128)} %get-tuple-element.256, ...), kind=kOutput, calls=%fused_computation.4.clone.1 | convolution fusion | flops 12913475584 | bytes 25430016 | tf_op jit(solution)/shard_map/while/body/eval_jaxpr/ts,psc->ptc/dot_general | solution.py:49
  106.5 2.3 bitcast_dynamic-update-slice_fusion.2
  108.9 32.6 %multiply_reduce_fusion.6 = (f32[256,4096]{1,0:T(8,128)S(1)}, f32[4,256,4096]{2,1,0:T(8,128)S(1)}) fusion(f32[4,4096]{1,0:T(4,128)S(1)} %dynamic-slice_bitcast_fusion.4, f32[256]{0:T(256)S(1)} %iota_convert_fusion.2, f32[4,4096]{1,0:T(4,128)S(1)} %neg.47, s32[256]{0:T(256)S(1)} %get-tuple-element.257, f32[256,4096]{1,0:T(8,128)} %get-tuple-element.256, ...), kind=kOutput, calls=%fused_computation.4.clone.1 | convolution fusion | flops 12913475584 | bytes 25430016 | tf_op jit(solution)/shard_map/while/body/eval_jaxpr/ts,psc->ptc/dot_general | solution.py:49
  141.6 2.3 bitcast_dynamic-update-slice_fusion.2
  144.0 32.6 %multiply_reduce_fusion.6 = (f32[256,4096]{1,0:T(8,128)S(1)}, f32[4,256,4096]{2,1,0:T(8,128)S(1)}) fusion(f32[4,4096]{1,0:T(4,128)S(1)} %dynamic-slice_bitcast_fusion.4, f32[256]{0:T(256)S(1)} %iota_convert_fusion.2, f32[4,4096]{1,0:T(4,128)S(1)} %neg.47, s32[256]{0:T(256)S(1)} %get-tuple-element.257, f32[256,4096]{1,0:T(8,128)} %get-tuple-element.256, ...), kind=kOutput, calls=%fused_computation.4.clone.1 | convolution fusion | flops 12913475584 | bytes 25430016 | tf_op jit(solution)/shard_map/while/body/eval_jaxpr/ts,psc->ptc/dot_general | solution.py:49
  179.1 140.8 %while.24 = (s32[]{:T(128)}, f32[16,4096]{1,0:T(8,128)S(1)}, f32[16,4096]{1,0:T(8,128)S(1)}, f32[16,4096]{1,0:T(8,128)S(1)}, s32[]{:T(128)}) while((s32[]{:T(128)}, f32[16,4096]{1,0:T(8,128)S(1)}, f32[16,4096]{1,0:T(8,128)S(1)}, f32[16,4096]{1,0:T(8,128)S(1)}, s32[]{:T(128)}) %tuple.65), condition=%wide.region_7.8_spmd, body=%wide.region_6.7_spmd.sunk | while | flops 131074 | bytes 2097253 | solution.py:62
  181.1 7.7 %collective-permute-done = f32[16,4096]{1,0:T(8,128)S(1)} collective-permute-done((f32[16,4096]{1,0:T(8,128)S(1)}, f32[16,4096]{1,0:T(8,128)S(1)}, u32[]{:S(2)}, u32[]{:S(2)}) %collective-permute-start) | collective-permute-done | bytes 262176 | tf_op jit(solution)/shard_map/while/body/eval_jaxpr/ppermute | solution.py:10
  190.7 6.8 %collective-permute-done = f32[16,4096]{1,0:T(8,128)S(1)} collective-permute-done((f32[16,4096]{1,0:T(8,128)S(1)}, f32[16,4096]{1,0:T(8,128)S(1)}, u32[]{:S(2)}, u32[]{:S(2)}) %collective-permute-start) | collective-permute-done | bytes 262176 | tf_op jit(solution)/shard_map/while/body/eval_jaxpr/ppermute | solution.py:10
  199.5 6.1 %collective-permute-done = f32[16,4096]{1,0:T(8,128)S(1)} collective-permute-done((f32[16,4096]{1,0:T(8,128)S(1)}, f32[16,4096]{1,0:T(8,128)S(1)}, u32[]{:S(2)}, u32[]{:S(2)}) %collective-permute-start) | collective-permute-done | bytes 262176 | tf_op jit(solution)/shard_map/while/body/eval_jaxpr/ppermute | solution.py:10
  207.6 6.1 %collective-permute-done = f32[16,4096]{1,0:T(8,128)S(1)} collective-permute-done((f32[16,4096]{1,0:T(8,128)S(1)}, f32[16,4096]{1,0:T(8,128)S(1)}, u32[]{:S(2)}, u32[]{:S(2)}) %collective-permute-start) | collective-permute-done | bytes 262176 | tf_op jit(solution)/shard_map/while/body/eval_jaxpr/ppermute | solution.py:10
  215.6 6.1 %collective-permute-done = f32[16,4096]{1,0:T(8,128)S(1)} collective-permute-done((f32[16,4096]{1,0:T(8,128)S(1)}, f32[16,4096]{1,0:T(8,128)S(1)}, u32[]{:S(2)}, u32[]{:S(2)}) %collective-permute-start) | collective-permute-done | bytes 262176 | tf_op jit(solution)/shard_map/while/body/eval_jaxpr/ppermute | solution.py:10
  223.7 6.4 %collective-permute-done = f32[16,4096]{1,0:T(8,128)S(1)} collective-permute-done((f32[16,4096]{1,0:T(8,128)S(1)}, f32[16,4096]{1,0:T(8,128)S(1)}, u32[]{:S(2)}, u32[]{:S(2)}) %collective-permute-start) | collective-permute-done | bytes 262176 | tf_op jit(solution)/shard_map/while/body/eval_jaxpr/ppermute | solution.py:10
  232.0 7.2 %collective-permute-done = f32[16,4096]{1,0:T(8,128)S(1)} collective-permute-done((f32[16,4096]{1,0:T(8,128)S(1)}, f32[16,4096]{1,0:T(8,128)S(1)}, u32[]{:S(2)}, u32[]{:S(2)}) %collective-permute-start) | collective-permute-done | bytes 262176 | tf_op jit(solution)/shard_map/while/body/eval_jaxpr/ppermute | solution.py:10
  241.2 8.1 %collective-permute-done = f32[16,4096]{1,0:T(8,128)S(1)} collective-permute-done((f32[16,4096]{1,0:T(8,128)S(1)}, f32[16,4096]{1,0:T(8,128)S(1)}, u32[]{:S(2)}, u32[]{:S(2)}) %collective-permute-start) | collective-permute-done | bytes 262176 | tf_op jit(solution)/shard_map/while/body/eval_jaxpr/ppermute | solution.py:10
  251.3 9.7 %collective-permute-done = f32[16,4096]{1,0:T(8,128)S(1)} collective-permute-done((f32[16,4096]{1,0:T(8,128)S(1)}, f32[16,4096]{1,0:T(8,128)S(1)}, u32[]{:S(2)}, u32[]{:S(2)}) %collective-permute-start) | collective-permute-done | bytes 262176 | tf_op jit(solution)/shard_map/while/body/eval_jaxpr/ppermute | solution.py:10
  263.0 10.2 %collective-permute-done = f32[16,4096]{1,0:T(8,128)S(1)} collective-permute-done((f32[16,4096]{1,0:T(8,128)S(1)}, f32[16,4096]{1,0:T(8,128)S(1)}, u32[]{:S(2)}, u32[]{:S(2)}) %collective-permute-start) | collective-permute-done | bytes 262176 | tf_op jit(solution)/shard_map/while/body/eval_jaxpr/ppermute | solution.py:10
  275.2 9.5 %collective-permute-done = f32[16,4096]{1,0:T(8,128)S(1)} collective-permute-done((f32[16,4096]{1,0:T(8,128)S(1)}, f32[16,4096]{1,0:T(8,128)S(1)}, u32[]{:S(2)}, u32[]{:S(2)}) %collective-permute-start) | collective-permute-done | bytes 262176 | tf_op jit(solution)/shard_map/while/body/eval_jaxpr/ppermute | solution.py:10
  286.6 7.3 %collective-permute-done = f32[16,4096]{1,0:T(8,128)S(1)} collective-permute-done((f32[16,4096]{1,0:T(8,128)S(1)}, f32[16,4096]{1,0:T(8,128)S(1)}, u32[]{:S(2)}, u32[]{:S(2)}) %collective-permute-start) | collective-permute-done | bytes 262176 | tf_op jit(solution)/shard_map/while/body/eval_jaxpr/ppermute | solution.py:10
  295.9 6.4 %collective-permute-done = f32[16,4096]{1,0:T(8,128)S(1)} collective-permute-done((f32[16,4096]{1,0:T(8,128)S(1)}, f32[16,4096]{1,0:T(8,128)S(1)}, u32[]{:S(2)}, u32[]{:S(2)}) %collective-permute-start) | collective-permute-done | bytes 262176 | tf_op jit(solution)/shard_map/while/body/eval_jaxpr/ppermute | solution.py:10
  304.2 6.7 %collective-permute-done = f32[16,4096]{1,0:T(8,128)S(1)} collective-permute-done((f32[16,4096]{1,0:T(8,128)S(1)}, f32[16,4096]{1,0:T(8,128)S(1)}, u32[]{:S(2)}, u32[]{:S(2)}) %collective-permute-start) | collective-permute-done | bytes 262176 | tf_op jit(solution)/shard_map/while/body/eval_jaxpr/ppermute | solution.py:10
  312.9 7.0 %collective-permute-done = f32[16,4096]{1,0:T(8,128)S(1)} collective-permute-done((f32[16,4096]{1,0:T(8,128)S(1)}, f32[16,4096]{1,0:T(8,128)S(1)}, u32[]{:S(2)}, u32[]{:S(2)}) %collective-permute-start) | collective-permute-done | bytes 262176 | tf_op jit(solution)/shard_map/while/body/eval_jaxpr/ppermute | solution.py:10
  320.0 9.8 %reduce_sum.72 = f32[256,4096]{1,0:T(8,128)} reduce(f32[4,256,4096]{2,1,0:T(8,128)} %get-tuple-element.70, f32[]{:T(128)} %constant.49.clone.1), dimensions={0}, to_apply=%region_5.6 | reduce | flops 3145728 | bytes 20971524 | tf_op jit(solution)/shard_map/reduce_sum | solution.py:54
  329.8 16.9 %multiply_reduce_fusion.4 = (f32[256,4096]{1,0:T(8,128)S(1)}, f32[256,4096]{1,0:T(8,128)S(1)}, f32[256,4096]{1,0:T(8,128)}, f32[256,4096]{1,0:T(8,128)}) fusion(f32[256]{0:T(256)S(1)} %convert_add_fusion, f32[4,4096]{1,0:T(4,128)S(1)} %get-tuple-element.149, f32[4,4096]{1,0:T(4,128)S(1)} %get-tuple-element.146, f32[4,4096]{1,0:T(4,128)S(1)} %get-tuple-element.148, ...), kind=kLoop, calls=%fused_computation.30 | loop fusion | flops 46137344 | bytes 17302528 | tf_op jit(solution)/shard_map/reduce_sum | solution.py:68
  346.7 9.0 %fusion.26 = bf16[256,4096]{1,0:T(8,128)(2,1)S(1)} fusion(f32[3,256,4096]{2,1,0:T(8,128)} %fusion.21, f32[256,4096]{1,0:T(8,128)} %get-tuple-element.116, f32[256,4096]{1,0:T(8,128)} %get-tuple-element.115, f32[256,4096]{1,0:T(8,128)S(1)} %get-tuple-element.114, f32[256,4096]{1,0:T(8,128)S(1)} %copy-done, f32[256,4096]{1,0:T(8,128)S(1)} %get-tuple-element.113, ...), kind=kLoop, calls=%fused_computation.43 | loop fusion | flops 13631488 | bytes 35668992 | tf_op jit(solution)/shard_map/convert_element_type | solution.py:69
  355.7 4.9 %convolution_convert_fusion = bf16[256,512]{1,0:T(8,128)(2,1)} fusion(bf16[256,4096]{1,0:T(8,128)(2,1)S(1)} %fusion.26, bf16[4096,512]{1,0:T(8,128)(2,1)} %param.19), kind=kOutput, calls=%fused_computation.44 | convolution fusion | flops 1073872896 | bytes 6553600 | tf_op jit(solution)/shard_map/dot_general | solution.py:70
  360.6 39.2 %all-reduce.2.cloned.1.call-done = bf16[256,512]{1,0:T(8,128)(2,1)} async-done(((bf16[256,512]{1,0:T(8,128)(2,1)}), bf16[256,512]{1,0:T(8,128)(2,1)}) %all-reduce.2.cloned.1.call-update) | async-done | bytes 262160 | tf_op jit(solution)/shard_map/psum | solution.py:72
  (96 shorter events, 47.2 us)
Async XLA Ops:
  7.2 392.7 %all-reduce.2.cloned.1.call-start = ((), (), s32[]{:S(2)}) async-start(), calls=%async_computation | async-start | bytes 524288 | tf_op jit(solution)/shard_map/psum | solution.py:72
  8.2 12.4 %collective-permute-start.1 = (bf16[3,2,4096]{2,1,0:T(2,128)(2,1)S(1)}, bf16[3,2,4096]{2,1,0:T(2,128)(2,1)S(1)}, u32[]{:S(2)}, u32[]{:S(2)}) collective-permute-start(bf16[3,2,4096]{2,1,0:T(2,128)(2,1)S(1)} %slice.85), channel_id=1, source_target_pairs={{0,2},{2,4},{4,6},{6,8},{8,10},{10,12},{12,14},{14,16},{16,18},{18... | collective-permute-start | bytes 147464 | tf_op jit(solution)/shard_map/ppermute | solution.py:10
  38.7 281.2 %copy-start.2 = (f32[16,4096]{1,0:T(8,128)S(1)}, f32[16,4096]{1,0:T(8,128)}, u32[]{:S(2)}) copy-start(f32[16,4096]{1,0:T(8,128)} %param.15) | copy-start | bytes 786436
  179.1 9.6 %collective-permute-start = (f32[16,4096]{1,0:T(8,128)S(1)}, f32[16,4096]{1,0:T(8,128)S(1)}, u32[]{:S(2)}, u32[]{:S(2)}) collective-permute-start(f32[16,4096]{1,0:T(8,128)S(1)} %multiply_add_fusion.2), channel_id=1, source_target_pairs={{0,2},{2,4},{4,6},{6,8},{8,10},{10,12},{12,14},{14,16},{16,18},{18... | collective-permute-start | bytes 786440 | tf_op jit(solution)/shard_map/while/body/eval_jaxpr/ppermute | solution.py:10
  188.8 8.7 %collective-permute-start = (f32[16,4096]{1,0:T(8,128)S(1)}, f32[16,4096]{1,0:T(8,128)S(1)}, u32[]{:S(2)}, u32[]{:S(2)}) collective-permute-start(f32[16,4096]{1,0:T(8,128)S(1)} %multiply_add_fusion.2), channel_id=1, source_target_pairs={{0,2},{2,4},{4,6},{6,8},{8,10},{10,12},{12,14},{14,16},{16,18},{18... | collective-permute-start | bytes 786440 | tf_op jit(solution)/shard_map/while/body/eval_jaxpr/ppermute | solution.py:10
  197.6 8.0 %collective-permute-start = (f32[16,4096]{1,0:T(8,128)S(1)}, f32[16,4096]{1,0:T(8,128)S(1)}, u32[]{:S(2)}, u32[]{:S(2)}) collective-permute-start(f32[16,4096]{1,0:T(8,128)S(1)} %multiply_add_fusion.2), channel_id=1, source_target_pairs={{0,2},{2,4},{4,6},{6,8},{8,10},{10,12},{12,14},{14,16},{16,18},{18... | collective-permute-start | bytes 786440 | tf_op jit(solution)/shard_map/while/body/eval_jaxpr/ppermute | solution.py:10
  205.6 8.0 %collective-permute-start = (f32[16,4096]{1,0:T(8,128)S(1)}, f32[16,4096]{1,0:T(8,128)S(1)}, u32[]{:S(2)}, u32[]{:S(2)}) collective-permute-start(f32[16,4096]{1,0:T(8,128)S(1)} %multiply_add_fusion.2), channel_id=1, source_target_pairs={{0,2},{2,4},{4,6},{6,8},{8,10},{10,12},{12,14},{14,16},{16,18},{18... | collective-permute-start | bytes 786440 | tf_op jit(solution)/shard_map/while/body/eval_jaxpr/ppermute | solution.py:10
  213.7 8.0 %collective-permute-start = (f32[16,4096]{1,0:T(8,128)S(1)}, f32[16,4096]{1,0:T(8,128)S(1)}, u32[]{:S(2)}, u32[]{:S(2)}) collective-permute-start(f32[16,4096]{1,0:T(8,128)S(1)} %multiply_add_fusion.2), channel_id=1, source_target_pairs={{0,2},{2,4},{4,6},{6,8},{8,10},{10,12},{12,14},{14,16},{16,18},{18... | collective-permute-start | bytes 786440 | tf_op jit(solution)/shard_map/while/body/eval_jaxpr/ppermute | solution.py:10
  221.7 8.3 %collective-permute-start = (f32[16,4096]{1,0:T(8,128)S(1)}, f32[16,4096]{1,0:T(8,128)S(1)}, u32[]{:S(2)}, u32[]{:S(2)}) collective-permute-start(f32[16,4096]{1,0:T(8,128)S(1)} %multiply_add_fusion.2), channel_id=1, source_target_pairs={{0,2},{2,4},{4,6},{6,8},{8,10},{10,12},{12,14},{14,16},{16,18},{18... | collective-permute-start | bytes 786440 | tf_op jit(solution)/shard_map/while/body/eval_jaxpr/ppermute | solution.py:10
  230.1 9.2 %collective-permute-start = (f32[16,4096]{1,0:T(8,128)S(1)}, f32[16,4096]{1,0:T(8,128)S(1)}, u32[]{:S(2)}, u32[]{:S(2)}) collective-permute-start(f32[16,4096]{1,0:T(8,128)S(1)} %multiply_add_fusion.2), channel_id=1, source_target_pairs={{0,2},{2,4},{4,6},{6,8},{8,10},{10,12},{12,14},{14,16},{16,18},{18... | collective-permute-start | bytes 786440 | tf_op jit(solution)/shard_map/while/body/eval_jaxpr/ppermute | solution.py:10
  239.3 10.0 %collective-permute-start = (f32[16,4096]{1,0:T(8,128)S(1)}, f32[16,4096]{1,0:T(8,128)S(1)}, u32[]{:S(2)}, u32[]{:S(2)}) collective-permute-start(f32[16,4096]{1,0:T(8,128)S(1)} %multiply_add_fusion.2), channel_id=1, source_target_pairs={{0,2},{2,4},{4,6},{6,8},{8,10},{10,12},{12,14},{14,16},{16,18},{18... | collective-permute-start | bytes 786440 | tf_op jit(solution)/shard_map/while/body/eval_jaxpr/ppermute | solution.py:10
  249.4 11.6 %collective-permute-start = (f32[16,4096]{1,0:T(8,128)S(1)}, f32[16,4096]{1,0:T(8,128)S(1)}, u32[]{:S(2)}, u32[]{:S(2)}) collective-permute-start(f32[16,4096]{1,0:T(8,128)S(1)} %multiply_add_fusion.2), channel_id=1, source_target_pairs={{0,2},{2,4},{4,6},{6,8},{8,10},{10,12},{12,14},{14,16},{16,18},{18... | collective-permute-start | bytes 786440 | tf_op jit(solution)/shard_map/while/body/eval_jaxpr/ppermute | solution.py:10
  261.0 12.1 %collective-permute-start = (f32[16,4096]{1,0:T(8,128)S(1)}, f32[16,4096]{1,0:T(8,128)S(1)}, u32[]{:S(2)}, u32[]{:S(2)}) collective-permute-start(f32[16,4096]{1,0:T(8,128)S(1)} %multiply_add_fusion.2), channel_id=1, source_target_pairs={{0,2},{2,4},{4,6},{6,8},{8,10},{10,12},{12,14},{14,16},{16,18},{18... | collective-permute-start | bytes 786440 | tf_op jit(solution)/shard_map/while/body/eval_jaxpr/ppermute | solution.py:10
  273.2 11.4 %collective-permute-start = (f32[16,4096]{1,0:T(8,128)S(1)}, f32[16,4096]{1,0:T(8,128)S(1)}, u32[]{:S(2)}, u32[]{:S(2)}) collective-permute-start(f32[16,4096]{1,0:T(8,128)S(1)} %multiply_add_fusion.2), channel_id=1, source_target_pairs={{0,2},{2,4},{4,6},{6,8},{8,10},{10,12},{12,14},{14,16},{16,18},{18... | collective-permute-start | bytes 786440 | tf_op jit(solution)/shard_map/while/body/eval_jaxpr/ppermute | solution.py:10
  284.7 9.2 %collective-permute-start = (f32[16,4096]{1,0:T(8,128)S(1)}, f32[16,4096]{1,0:T(8,128)S(1)}, u32[]{:S(2)}, u32[]{:S(2)}) collective-permute-start(f32[16,4096]{1,0:T(8,128)S(1)} %multiply_add_fusion.2), channel_id=1, source_target_pairs={{0,2},{2,4},{4,6},{6,8},{8,10},{10,12},{12,14},{14,16},{16,18},{18... | collective-permute-start | bytes 786440 | tf_op jit(solution)/shard_map/while/body/eval_jaxpr/ppermute | solution.py:10
  293.9 8.3 %collective-permute-start = (f32[16,4096]{1,0:T(8,128)S(1)}, f32[16,4096]{1,0:T(8,128)S(1)}, u32[]{:S(2)}, u32[]{:S(2)}) collective-permute-start(f32[16,4096]{1,0:T(8,128)S(1)} %multiply_add_fusion.2), channel_id=1, source_target_pairs={{0,2},{2,4},{4,6},{6,8},{8,10},{10,12},{12,14},{14,16},{16,18},{18... | collective-permute-start | bytes 786440 | tf_op jit(solution)/shard_map/while/body/eval_jaxpr/ppermute | solution.py:10
  302.3 8.6 %collective-permute-start = (f32[16,4096]{1,0:T(8,128)S(1)}, f32[16,4096]{1,0:T(8,128)S(1)}, u32[]{:S(2)}, u32[]{:S(2)}) collective-permute-start(f32[16,4096]{1,0:T(8,128)S(1)} %multiply_add_fusion.2), channel_id=1, source_target_pairs={{0,2},{2,4},{4,6},{6,8},{8,10},{10,12},{12,14},{14,16},{16,18},{18... | collective-permute-start | bytes 786440 | tf_op jit(solution)/shard_map/while/body/eval_jaxpr/ppermute | solution.py:10
  311.0 8.9 %collective-permute-start = (f32[16,4096]{1,0:T(8,128)S(1)}, f32[16,4096]{1,0:T(8,128)S(1)}, u32[]{:S(2)}, u32[]{:S(2)}) collective-permute-start(f32[16,4096]{1,0:T(8,128)S(1)} %multiply_add_fusion.2), channel_id=1, source_target_pairs={{0,2},{2,4},{4,6},{6,8},{8,10},{10,12},{12,14},{14,16},{16,18},{18... | collective-permute-start | bytes 786440 | tf_op jit(solution)/shard_map/while/body/eval_jaxpr/ppermute | solution.py:10
  329.8 16.9 %copy-start = (f32[256,4096]{1,0:T(8,128)S(1)}, f32[256,4096]{1,0:T(8,128)}, u32[]{:S(2)}) copy-start(f32[256,4096]{1,0:T(8,128)} %reduce_sum.72) | copy-start | bytes 12582916
  329.8 16.9 %copy-start.3 = (f32[4096]{0:T(1024)S(1)}, f32[4096]{0:T(1024)}, u32[]{:S(2)}) copy-start(f32[4096]{0:T(1024)} %param.16) | copy-start | bytes 49156
  329.8 16.9 %copy-start.4 = (f32[256]{0:T(256)S(1)}, f32[256]{0:T(256)}, u32[]{:S(2)}) copy-start(f32[256]{0:T(256)} %get-tuple-element.154) | copy-start | bytes 3076
  346.7 54.2 %copy-start.5 = (s32[256]{0:T(256)S(1)}, s32[256]{0:T(256)}, u32[]{:S(2)}) copy-start(s32[256]{0:T(256)} %param.18) | copy-start | bytes 3076
  355.7 47.1 %copy-start.1 = (bf16[256,4096]{1,0:T(8,128)(2,1)}, bf16[256,4096]{1,0:T(8,128)(2,1)S(1)}, u32[]{:S(2)}) copy-start(bf16[256,4096]{1,0:T(8,128)(2,1)S(1)} %fusion.26) | copy-start | bytes 6291460
Sparse Core Ops, SparseCore 0:
  360.7 39.0 all-reduce.1
where the time goes:
time: 412 us; the launch traced here: 410 us
  waiting for transfers between devices  150 us (36%)
  matrix products  135 us (33%)
  other arithmetic  61.9 us (15%)
  starting transfers between devices  32 us (8%)
  between operations  14.9 us (4%)
  local copies, waits for them, and re-layouts  14.8 us (4%)
    dot_general x4, matrix products, block_states(): jnp.einsum('ts,psc->ptc', same_doc, weighted, precision=lax.Precision.HIG...  130 us
    ppermute x16, waiting for transfers between devices, shifted(): return lax.ppermute(block, axis, route)  111 us
    psum x1, waiting for transfers between devices, local(): lax.psum(partial_logits.astype(jnp.bfloat16), 'chan').astype(jnp.float32)  39.2 us
    ppermute x16, starting transfers between devices, shifted(): return lax.ppermute(block, axis, route)  31.9 us
    reduce_sum x1, other arithmetic, local(): jnp.sum(weight_in[:, None, :] * fading, axis=0)  16.9 us
    reduce_sum x1, other arithmetic, local(): long_out = jnp.sum(partial_out, axis=0)  9.83 us
    dynamic_update_slice x8, local copies, waits for them, and re-layouts, local(): lax.map(block_states, (rate_groups, residue_groups))  9.23 us
    convert_element_type x1, other arithmetic, local(): (q_stream * (long_out + direct[None, :] * driver)).astype(jnp.bfloat16)  8.97 us
  transfers between devices with their start and end apart: 17, of which 16 were waited for; matrix products, arithmetic and copies ran while one was open for 2% of the time, Pallas kernels for 0%

commit v1 on v0

v1 whole, which is shorter than its diff:
```python
import functools

import jax
import jax.numpy as jnp
from jax import lax
from jax.experimental import pallas as pl
from jax.experimental.pallas import tpu as pltpu
from jax.sharding import PartitionSpec as P

MESH = pl.DeviceIdType.MESH
LANES = 128
GROUP = 8 * LANES
VMEM_LIMIT = 48 * 1024 * 1024


def doc_firsts(lengths_ref):
    firsts = [jnp.int32(0)]
    for d in range(lengths_ref.shape[0] - 1):
        firsts.append(firsts[-1] + lengths_ref[d])
    return firsts


def any_between(firsts, low, high):
    found = jnp.bool_(False)
    for first in firsts:
        found = found | ((first >= low) & (first < high))
    return found


def greet(peers):
    barrier = pltpu.get_barrier_semaphore()
    for axis, peer, there in peers:

        @pl.when(there)
        def _():
            pl.semaphore_signal(barrier, inc=1, device_id={axis: peer}, device_id_type=MESH)

    if peers:
        pl.semaphore_wait(barrier, sum(jnp.where(there, 1, 0) for _, _, there in peers))


def edge_kernel(blocks, tail_ref, out_ref, packed, landed, send_sem, recv_sem):
    me = lax.axis_index("seq")
    half = packed.shape[1]
    greet((("seq", me + 1, me < blocks - 1), ("seq", me - 1, me > 0)))
    rows = []
    for side in range(2):
        cols = pl.ds(side * half, half)
        for j in range(3):
            rows.append(tail_ref[j, :, cols].astype(jnp.float32)[14:16])
        rows.append(jnp.zeros((2, half), jnp.float32))
    packed[...] = jnp.concatenate(rows, axis=0).astype(jnp.bfloat16)
    copy = pltpu.make_async_remote_copy(
        src_ref=packed,
        dst_ref=landed,
        send_sem=send_sem,
        recv_sem=recv_sem,
        device_id={"seq": me + 1},
        device_id_type=MESH,
    )

    @pl.when(me < blocks - 1)
    def _():
        copy.start()

    @pl.when(me > 0)
    def _():
        copy.wait_recv()
        got = landed[...].astype(jnp.float32)
        out_ref[:, pl.ds(0, half)] = got[0:8]
        out_ref[:, pl.ds(half, half)] = got[8:16]

    @pl.when(me == 0)
    def _():
        out_ref[...] = jnp.zeros_like(out_ref)

    @pl.when(me < blocks - 1)
    def _():
        copy.wait_send()


def load_extended(ext, stream_ref, edge_ref, stream_id):
    block_len = stream_ref.shape[1]
    pitch = block_len + 8
    for ct in range(8):
        edge = edge_ref[:, pl.ds(ct * LANES, LANES)]
        both = jnp.concatenate([edge[0:6], edge[2 * stream_id : 2 * stream_id + 2]], axis=0)
        ext[pl.ds(ct * pitch, 8), :] = both

    def step(i, _):
        rows = pl.ds(pl.multiple_of(i * 16, 16), 16)
        for ct in range(8):
            tile = stream_ref[0, rows, pl.ds(ct * LANES, LANES)].astype(jnp.float32)
            ext[pl.ds(pl.multiple_of(ct * pitch + i * 16 + 8, 8), 16), :] = tile
        return 0

    lax.fori_loop(0, block_len // 16, step, 0)


def taps_of(ext, filter_ref, stream_id, i, ct, masks):
    cols = pl.ds(ct * LANES, LANES)
    pitch = ext.shape[0] // 8
    terms = []
    for shift in range(3):
        tap = filter_ref[stream_id, shift : shift + 1, cols]
        rows = pl.ds(ct * pitch + i * 8 + (8 - shift), 8)
        term = tap * ext[rows, :]
        if shift and masks is not None:
            term = jnp.where(masks[shift - 1], term, 0.0)
        terms.append(term)
    return terms[0] + terms[1] + terms[2]


def tile_masks(firsts, base):
    pos = base + lax.broadcasted_iota(jnp.int32, (8, LANES), 0)
    start = jnp.zeros((8, LANES), jnp.int32)
    for first in firsts:
        start = jnp.maximum(start, jnp.where(first <= pos, first, 0))
    return [pos - shift >= start for shift in (1, 2)]


def to_sublanes(ref, scratch, row_count):
    for top in range(0, row_count, 8):
        for ct in range(8):
            scratch[pl.ds(top * 8 + ct * 8, 8), :] = ref[top : top + 8, pl.ds(ct * LANES, LANES)]
    return [scratch[pl.ds((p // 8) * 64 + p % 8, 8, stride=8), :] for p in range(row_count)]


def local_kernel(
    lengths_ref, k_ref, v_ref, edge_ref, filter_ref, rate_ref, residue_ref, direct_ref,
    y_ref, end_ref, rate_out, weight_out,
    ext_k, ext_v, turn, driver,
):
    block_len = k_ref.shape[1]
    poles = rate_ref.shape[0]
    first_pos = lax.axis_index("seq") * block_len
    firsts = doc_firsts(lengths_ref)
    load_extended(ext_k, k_ref, edge_ref, 1)
    load_extended(ext_v, v_ref, edge_ref, 2)

    def filter_step(i, _):
        base = first_pos + i * 8

        def fill(masks):
            for ct in range(8):
                k = taps_of(ext_k, filter_ref, 1, i, ct, masks)
                v = taps_of(ext_v, filter_ref, 2, i, ct, masks)
                driver[pl.ds(pl.multiple_of(i * 64 + ct * 8, 8), 8), :] = k * v

        near = any_between(firsts, base - 1, base + 8)

        @pl.when(near)
        def _():
            fill(tile_masks(firsts, base))

        @pl.when(jnp.logical_not(near))
        def _():
            fill(None)

        return 0

    lax.fori_loop(0, block_len // 8, filter_step, 0)

    rates = to_sublanes(rate_ref, turn, poles)
    decays = [jnp.exp(-r) for r in rates]
    for p in range(poles):
        rate_out[p, 0] = rates[p]
    residues = to_sublanes(residue_ref, turn, poles)
    weights = [residues[p] * (1.0 - decays[p]) for p in range(poles)]
    for p in range(poles):
        weight_out[p, 0] = weights[p]
    for ct in range(8):
        turn[pl.ds(ct * 8, 8), :] = jnp.broadcast_to(direct_ref[:, pl.ds(ct * LANES, LANES)], (8, LANES))
    direct = turn[pl.ds(0, 8, stride=8), :]

    def chunk(i, states):
        base = first_pos + i * 8

        def run(states, with_reset):
            states = list(states)
            for j in range(8):
                x = driver[pl.ds(i * 64 + j, 8, stride=8), :]
                if with_reset:
                    hit = any_between(firsts, base + j, base + j + 1)
                    keep = jnp.where(hit, 0.0, 1.0)
                sums = [direct * x, None, None, None]
                for p in range(poles):
                    held = states[p] * keep if with_reset else states[p]
                    states[p] = decays[p] * held + x
                    term = weights[p] * states[p]
                    sums[p % 4] = term if sums[p % 4] is None else sums[p % 4] + term
                y_ref[0, pl.ds(i * 64 + j, 8, stride=8), :] = (sums[0] + sums[1]) + (sums[2] + sums[3])
            return tuple(states)

        return lax.cond(
            any_between(firsts, base, base + 8),
            lambda s: run(s, True),
            lambda s: run(s, False),
            states,
        )

    zeros = tuple(jnp.zeros((8, LANES), jnp.float32) for _ in range(poles))
    states = lax.fori_loop(0, block_len // 8, chunk, zeros)
    for p in range(poles):
        end_ref[p, 0] = states[p]


def exchange_kernel(blocks, block_len, pieces, lengths_ref, rate_ref, end_ref, in_ref, outbox, inbox, send_sem, recv_sem):
    me = lax.axis_index("seq")
    first_pos = me * block_len
    rounds = max(1, (blocks - 1).bit_length())
    peers = []
    for k in range(rounds):
        peers.append(("seq", me + (1 << k), me + (1 << k) < blocks))
        peers.append(("seq", me - (1 << k), me >= (1 << k)))
    greet(peers)
    firsts = doc_firsts(lengths_ref)

    def last_start(pos):
        best = jnp.int32(0)
        for first in firsts:
            best = jnp.maximum(best, jnp.where(first <= pos, first, 0))
        return best

    own_keep = jnp.where(last_start(first_pos + block_len - 1) < first_pos, 1.0, 0.0)
    span = end_ref.shape[0] // pieces

    def copy(k, piece):
        rows = pl.ds(piece * span, span)
        return pltpu.make_async_remote_copy(
            src_ref=outbox.at[k, rows],
            dst_ref=inbox.at[k, rows],
            send_sem=send_sem.at[k, piece],
            recv_sem=recv_sem.at[k, piece],
            device_id={"seq": me + (1 << k)},
            device_id_type=MESH,
        )

    in_ref[...] = jnp.zeros_like(in_ref)
    for k in range(rounds):
        reach = 1 << k
        far = first_pos - (reach - 1) * block_len
        for piece in range(pieces):
            rows = pl.ds(piece * span, span)

            @pl.when(me + reach < blocks)
            def _():
                whole = end_ref[rows, :]
                if k:
                    fade = jnp.exp(-rate_ref[rows, :] * float(block_len)) * own_keep
                    whole = whole + fade * in_ref[rows, :]
                outbox[k, rows, :] = whole.astype(jnp.bfloat16)
                copy(k, piece).start()

        if k:
            clear = jnp.where(last_start(first_pos - 1) < far, 1.0, 0.0)
        for piece in range(pieces):
            rows = pl.ds(piece * span, span)

            @pl.when(me >= reach)
            def _():
                copy(k, piece).wait_recv()
                got = inbox[k, rows, :].astype(jnp.float32)
                if k:
                    fade = jnp.exp(-rate_ref[rows, :] * float((reach - 1) * block_len))
                    got = got * (fade * clear)
                in_ref[rows, :] += got

    for k in range(rounds):
        for piece in range(pieces):

            @pl.when(me + (1 << k) < blocks)
            def _():
                copy(k, piece).wait_send()


def finish_kernel(
    lengths_ref, q_ref, edge_ref, filter_ref, rate_ref, weight_ref, in_ref, y_in, unembed_ref,
    gated_ref, logits_ref,
    ext_q, y, total,
):
    block_len = q_ref.shape[1]
    poles = rate_ref.shape[0]
    first_pos = lax.axis_index("seq") * block_len
    firsts = doc_firsts(lengths_ref)
    group = pl.program_id(0)
    cut = jnp.int32(block_len)
    for first in firsts:
        cut = jnp.where(first >= first_pos, jnp.minimum(cut, first - first_pos), cut)
    load_extended(ext_q, q_ref, edge_ref, 0)
    decays = [jnp.exp(-rate_ref[p, 0]) for p in range(poles)]
    fading = tuple(weight_ref[p, 0] * in_ref[p, 0] * decays[p] for p in range(poles))

    def fade_chunk(i, fading):
        fading = list(fading)
        for j in range(8):
            sums = [fading[0], fading[1], fading[2], fading[3]]
            for p in range(4, poles):
                sums[p % 4] = sums[p % 4] + fading[p]
            arrived = (sums[0] + sums[1]) + (sums[2] + sums[3])
            rows = pl.ds(i * 64 + j, 8, stride=8)
            y[rows, :] = y_in[0, rows, :] + jnp.where(i * 8 + j < cut, 1.0, 0.0) * arrived
            fading = [f * d for f, d in zip(fading, decays)]
        return tuple(fading)

    carried = (cut + 7) // 8
    lax.fori_loop(0, carried, fade_chunk, fading)

    def plain_chunk(i, _):
        rows = pl.ds(pl.multiple_of(i * 64, 64), 64)
        y[rows, :] = y_in[0, rows, :]
        return 0

    lax.fori_loop(carried, block_len // 8, plain_chunk, 0)

    def gate_step(i, _):
        base = first_pos + i * 16

        def fill(masked):
            for ct in range(8):
                halves = []
                for side in range(2):
                    tile = i * 2 + side
                    masks = tile_masks(firsts, base + side * 8) if masked else None
                    q = taps_of(ext_q, filter_ref, 0, tile, ct, masks)
                    halves.append(q * y[pl.ds(pl.multiple_of(tile * 64 + ct * 8, 8), 8), :])
                both = jnp.concatenate(halves, axis=0).astype(jnp.bfloat16)
                gated_ref[pl.ds(pl.multiple_of(i * 16, 16), 16), pl.ds(ct * LANES, LANES)] = both

        near = any_between(firsts, base - 1, base + 16)

        @pl.when(near)
        def _():
            fill(True)

        @pl.when(jnp.logical_not(near))
        def _():
            fill(False)

        return 0

    lax.fori_loop(0, block_len // 16, gate_step, 0)
    part = jnp.dot(gated_ref[...], unembed_ref[...], preferred_element_type=jnp.float32)

    @pl.when(group == 0)
    def _():
        total[...] = part

    @pl.when(group > 0)
    def _():
        total[...] += part

    @pl.when(group == pl.num_programs(0) - 1)
    def _():
        logits_ref[...] = total[...].astype(jnp.bfloat16)


def loss_kernel(parts, logits_ref, target_ref, loss_ref, inbox, send_sem, recv_sem):
    me = lax.axis_index("chan")
    others = [lax.rem(me + d, parts) for d in range(1, parts)]
    greet([("chan", other, me >= 0) for other in others])
    copies = []
    for d in range(1, parts):
        copies.append(
            pltpu.make_async_remote_copy(
                src_ref=logits_ref,
                dst_ref=inbox.at[me],
                send_sem=send_sem.at[d - 1],
                recv_sem=recv_sem.at[d - 1],
                device_id={"chan": others[d - 1]},
                device_id_type=MESH,
            )
        )
        copies[-1].start()
    inbox[me] = logits_ref[...]
    for copy in copies:
        copy.wait_recv()
    block_len, vocab = logits_ref.shape
    eye = lax.broadcasted_iota(jnp.int32, (LANES, LANES), 0) == lax.broadcasted_iota(
        jnp.int32, (LANES, LANES), 1
    )
    vocab_ids = lax.broadcasted_iota(jnp.int32, (LANES, vocab), 1)
    for tile in range(block_len // LANES):
        rows = pl.ds(tile * LANES, LANES)
        logits = inbox[0, rows, :].astype(jnp.float32)
        for part in range(1, parts):
            logits = logits + inbox[part, rows, :].astype(jnp.float32)
        wanted = jnp.where(eye, target_ref[tile : tile + 1, :].astype(jnp.float32), 0.0)
        wanted = jnp.sum(wanted, axis=1, keepdims=True).astype(jnp.int32)
        peak = jnp.max(logits, axis=1, keepdims=True)
        exp_total = jnp.sum(jnp.exp(logits - peak), axis=1, keepdims=True)
        picked = jnp.sum(jnp.where(vocab_ids == wanted, logits, 0.0), axis=1, keepdims=True)
        loss = peak + jnp.log(exp_total) - picked
        loss_ref[tile : tile + 1, :] = jnp.sum(jnp.where(eye, loss, 0.0), axis=0, keepdims=True)
    for copy in copies:
        copy.wait_send()


def local(blocks, parts, streams, short_filter, pole_rates, residues, direct, doc_lengths, targets, unembed):
    block_len, chans = streams.shape[1], streams.shape[2]
    poles, vocab = pole_rates.shape[0], unembed.shape[1]
    groups = chans // GROUP
    f32, bf16 = jnp.float32, jnp.bfloat16
    shape = jax.ShapeDtypeStruct
    vmem = pl.BlockSpec(memory_space=pltpu.VMEM)
    smem = pl.BlockSpec(memory_space=pltpu.SMEM)
    params = functools.partial(pltpu.CompilerParams, vmem_limit_bytes=VMEM_LIMIT)

    edges = pl.pallas_call(
        functools.partial(edge_kernel, blocks),
        name="edges",
        grid=(1,),
        out_shape=shape((8, chans), f32),
        in_specs=[pl.BlockSpec((3, 16, chans), lambda g: (0, block_len // 16 - 1, 0))],
        out_specs=pl.BlockSpec((8, chans), lambda g: (0, 0)),
        scratch_shapes=[
            pltpu.VMEM((16, chans // 2), bf16),
            pltpu.VMEM((16, chans // 2), bf16),
            pltpu.SemaphoreType.DMA,
            pltpu.SemaphoreType.DMA,
        ],
        compiler_params=params(collective_id=0, has_side_effects=True),
    )(streams)

    def stream_spec(j):
        return pl.BlockSpec((1, block_len, GROUP), lambda g: (j, 0, g))

    edge_spec = pl.BlockSpec((8, GROUP), lambda g: (0, g))
    filter_spec = pl.BlockSpec((3, 3, GROUP), lambda g: (0, 0, g))
    pole_spec = pl.BlockSpec((poles, GROUP), lambda g: (0, g))
    turned_spec = pl.BlockSpec((poles, 1, 8, LANES), lambda g: (0, g, 0, 0))
    y_spec = pl.BlockSpec((1, block_len * 8, LANES), lambda g: (g, 0, 0))
    turned = shape((poles, groups, 8, LANES), f32)

    y_local, ends, rates, weights = pl.pallas_call(
        local_kernel,
        name="recur",
        grid=(groups,),
        out_shape=[shape((groups, block_len * 8, LANES), f32), turned, turned, turned],
        in_specs=[
            smem, stream_spec(1), stream_spec(2), edge_spec, filter_spec, pole_spec, pole_spec,
            pl.BlockSpec((1, GROUP), lambda g: (0, g)),
        ],
        out_specs=[y_spec, turned_spec, turned_spec, turned_spec],
        scratch_shapes=[
            pltpu.VMEM((8 * (block_len + 8), LANES), f32),
            pltpu.VMEM((8 * (block_len + 8), LANES), f32),
            pltpu.VMEM((poles * 8, LANES), f32),
            pltpu.VMEM((block_len * 8, LANES), f32),
        ],
        compiler_params=params(),
    )(doc_lengths, streams, streams, edges, short_filter, pole_rates, residues, direct.reshape(1, chans))

    rounds = max(1, (blocks - 1).bit_length())
    rows = poles * groups * 8
    pieces = 2
    incoming = pl.pallas_call(
        functools.partial(exchange_kernel, blocks, block_len, pieces),
        name="exchange",
        out_shape=shape((rows, LANES), f32),
        in_specs=[smem, vmem, vmem],
        out_specs=vmem,
        scratch_shapes=[
            pltpu.VMEM((rounds, rows, LANES), bf16),
            pltpu.VMEM((rounds, rows, LANES), bf16),
            pltpu.SemaphoreType.DMA((rounds, pieces)),
            pltpu.SemaphoreType.DMA((rounds, pieces)),
        ],
        compiler_params=params(collective_id=1, has_side_effects=True),
    )(doc_lengths, rates.reshape(rows, LANES), ends.reshape(rows, LANES))

    gated_out, logits = pl.pallas_call(
        finish_kernel,
        name="finish",
        grid=(groups,),
        out_shape=[shape((block_len, chans), bf16), shape((block_len, vocab), bf16)],
        in_specs=[
            smem, stream_spec(0), edge_spec, filter_spec, turned_spec, turned_spec, turned_spec, y_spec,
            pl.BlockSpec((GROUP, vocab), lambda g: (g, 0)),
        ],
        out_specs=[
            pl.BlockSpec((block_len, GROUP), lambda g: (0, g)),
            pl.BlockSpec((block_len, vocab), lambda g: (0, 0)),
        ],
        scratch_shapes=[
            pltpu.VMEM((8 * (block_len + 8), LANES), f32),
            pltpu.VMEM((block_len * 8, LANES), f32),
            pltpu.VMEM((block_len, vocab), f32),
        ],
        compiler_params=params(),
    )(
        doc_lengths, streams, edges, short_filter, rates, weights,
        incoming.reshape(turned.shape), y_local, unembed,
    )

    loss = pl.pallas_call(
        functools.partial(loss_kernel, parts),
        name="loss",
        out_shape=shape((block_len // LANES, LANES), f32),
        in_specs=[vmem, vmem],
        out_specs=vmem,
        scratch_shapes=[
            pltpu.VMEM((parts, block_len, vocab), bf16),
            pltpu.SemaphoreType.DMA((max(1, parts - 1),)),
            pltpu.SemaphoreType.DMA((max(1, parts - 1),)),
        ],
        compiler_params=params(collective_id=2, has_side_effects=True),
    )(logits, targets.reshape(block_len // LANES, LANES))
    return gated_out, loss.reshape(block_len)


def solution(mesh):
    in_specs = (
        P(None, "seq", "chan"),
        P(None, None, "chan"),
        P(None, "chan"),
        P(None, "chan"),
        P("chan"),
        P(),
        P("seq"),
        P("chan", None),
    )
    out_specs = (P("seq", "chan"), P("seq"))
    body = functools.partial(local, mesh.shape["seq"], mesh.shape["chan"])
    return jax.shard_map(body, mesh=mesh, in_specs=in_specs, out_specs=out_specs, check_vma=False)
```

time: 412 us -> 63.5 us (0.15)
  waiting for transfers between devices: 150 us -> 0 us
  matrix products: 135 us -> 0 us
  Pallas kernels: 0 us -> 62 us
  other arithmetic: 61.9 us -> 0 us
  starting transfers between devices: 32 us -> 0 us
  local copies, waits for them, and re-layouts: 14.8 us -> 0.59 us
  between operations: 14.9 us -> 0.75 us
    dot_general x5 -> x0, matrix products: 135 us -> none  [the longest x4 130 us: block_states(): jnp.einsum('ts,psc->ptc', same_doc, weighted, precision=lax.Precision.HIG...]
    ppermute x16 -> x0, waiting for transfers between devices: 111 us -> none  [shifted(): return lax.ppermute(block, axis, route)]
    pallas_call x0 -> x5, Pallas kernels: none -> 62 us  [the longest x1 20.2 us: local(): pl.pallas_call(local_kernel, name='recur', grid=(groups,), out_shape=[sha...]
    psum x1 -> x0, waiting for transfers between devices: 39.2 us -> none  [local(): lax.psum(partial_logits.astype(jnp.bfloat16), 'chan').astype(jnp.float32)]
    ppermute x16 -> x0, starting transfers between devices: 31.9 us -> none  [shifted(): return lax.ppermute(block, axis, route)]
    reduce_sum x3 -> x0, other arithmetic: 28 us -> none  [the longest x1 16.9 us: local(): jnp.sum(weight_in[:, None, :] * fading, axis=0)]
    convert_element_type x7 -> x0, other arithmetic: 14.3 us -> none  [the longest x1 8.97 us: local(): (q_stream * (long_out + direct[None, :] * driver)).astype(jnp.bfloat16)]
    dynamic_update_slice x8 -> x0, local copies, waits for them, and re-layouts: 9.23 us -> none  [local(): lax.map(block_states, (rate_groups, residue_groups))]
  transfers between devices with their start and end apart: 17 -> 0, of which waited for: 16 -> 0; matrix products, arithmetic and copies ran while one was open for 2% -> 0% of each run, Pallas kernels for 0% -> 0%
where the time goes in v1:
time: 63.5 us; the launch traced here: 63.3 us
  Pallas kernels  62 us (98%)
  between operations  0.75 us (1%)
    pallas_call x1, Pallas kernels, local(): pl.pallas_call(local_kernel, name='recur', grid=(groups,), out_shape=[sha...  20.2 us
    pallas_call x1, Pallas kernels, local(): pl.pallas_call(functools.partial(exchange_kernel, blocks, block_len, piec...  19.8 us
    pallas_call x1, Pallas kernels, local(): pl.pallas_call(finish_kernel, name='finish', grid=(groups,), out_shape=[s...  12.9 us
    pallas_call x1, Pallas kernels, local(): pl.pallas_call(functools.partial(edge_kernel, blocks), name='edges', grid...  5.16 us
    pallas_call x1, Pallas kernels, local(): pl.pallas_call(functools.partial(loss_kernel, parts), name='loss', out_sh...  3.92 us

profile of v1, /device:TPU:29, one launch (start us, length us, event | category | flops | bytes accessed | tf_op | source)
XLA Modules:
  0.0 63.3 jit_solution(9064873441279867648)
XLA Ops:
  0.6 0.0 copy-start.4
  0.6 0.0 copy-start
  0.7 0.0 copy-start.3
  0.7 0.0 copy-start.2
  0.7 0.0 copy-start.1
  0.7 5.2 %edges.1.edge_ref = f32[8,4096]{1,0:T(8,128)S(1)} custom-call(bf16[3,256,4096]{2,1,0:T(8,128)(2,1)} %q_ref.1), custom_call_target="tpu_custom_call" | custom-call | tf_op jit(solution)/shard_map/edges/pallas_call | solution.py:409
  5.9 0.0 copy-done.4
  5.9 0.0 copy-done
  5.9 0.0 copy-done.3
  5.9 0.0 copy-done.2
  5.9 0.0 copy-done.1
  5.9 20.2 %recur.1 = (f32[4,2048,128]{2,1,0:T(8,128)S(1)}, f32[16,4,8,128]{3,2,1,0:T(8,128)S(1)}, f32[16,4,8,128]{3,2,1,0:T(8,128)S(1)}, f32[16,4,8,128]{3,2,1,0:T(8,128)S(1)}) custom-call(s32[4]{0:T(128)S(1)} %copy-done.4, bf16[3,256,4096]{2,1,0:T(8,128)(2,1)} %q_ref.1, bf16[3,256,4096]{2,1,0:T(8,128)(2,1)} %q_ref.1, f32[8,4096]{1,0:T(8,128)S(1)} %edges.1.edge_ref, ...), custom_call_target="tpu_custom_call" | custom-call | tf_op jit(solution)/shard_map/recur/pallas_call | solution.py:435
  26.1 19.8 %exchange.1 = f32[512,128]{1,0:T(8,128)S(1)} custom-call(s32[4]{0:T(128)S(1)} %copy-done.4, f32[512,128]{1,0:T(8,128)S(1)} %bitcast.6, f32[512,128]{1,0:T(8,128)S(1)} %bitcast.8), custom_call_target="tpu_custom_call" | custom-call | tf_op jit(solution)/shard_map/exchange/pallas_call | solution.py:457
  45.9 0.0 copy-start.5
  45.9 12.9 %finish.1 = (bf16[256,4096]{1,0:T(8,128)(2,1)}, bf16[256,512]{1,0:T(8,128)(2,1)S(1)}) custom-call(s32[4]{0:T(128)S(1)} %copy-done.4, bf16[3,256,4096]{2,1,0:T(8,128)(2,1)} %q_ref.1, f32[8,4096]{1,0:T(8,128)S(1)} %edges.1.edge_ref, f32[3,3,4096]{2,1,0:T(4,128)S(1)} %copy-done, f32[16,4,8,128]{3,2,1,0:T(8,128)S(1)} %get-tuple-element.8.rate_ref, ...), custom_call_target="tpu_custom_call" | custom-call | tf_op jit(solution)/shard_map/finish/pallas_call | solution.py:472
  58.8 0.0 copy-done.5
  58.8 3.9 %loss.1 = f32[2,128]{1,0:T(2,128)S(1)} custom-call(bf16[256,512]{1,0:T(8,128)(2,1)S(1)} %get-tuple-element.13.logits_ref, s32[2,128]{1,0:T(2,128)S(1)} %bitcast.11), custom_call_target="tpu_custom_call" | custom-call | tf_op jit(solution)/shard_map/loss/pallas_call | solution.py:496
  62.8 0.6 copy.11
Async XLA Ops:
  0.6 5.2 %copy-start.4 = (s32[4]{0:T(128)S(1)}, s32[4]{0:T(128)}, u32[]{:S(2)}) copy-start(s32[4]{0:T(128)} %lengths_ref.5) | copy-start | bytes 52
  0.6 5.2 %copy-start = (f32[3,3,4096]{2,1,0:T(4,128)S(1)}, f32[3,3,4096]{2,1,0:T(4,128)}, u32[]{:S(2)}) copy-start(f32[3,3,4096]{2,1,0:T(4,128)} %filter_ref.3) | copy-start | bytes 442372
  0.7 5.2 %copy-start.3 = (f32[4096]{0:T(1024)S(1)}, f32[4096]{0:T(1024)}, u32[]{:S(2)}) copy-start(f32[4096]{0:T(1024)} %param.12) | copy-start | bytes 49156
  0.7 5.2 %copy-start.2 = (f32[16,4096]{1,0:T(8,128)S(1)}, f32[16,4096]{1,0:T(8,128)}, u32[]{:S(2)}) copy-start(f32[16,4096]{1,0:T(8,128)} %residue_ref.1) | copy-start | bytes 786436
  0.7 5.2 %copy-start.1 = (f32[16,4096]{1,0:T(8,128)S(1)}, f32[16,4096]{1,0:T(8,128)}, u32[]{:S(2)}) copy-start(f32[16,4096]{1,0:T(8,128)} %rate_ref.1) | copy-start | bytes 786436
  45.9 12.9 %copy-start.5 = (s32[256]{0:T(256)S(1)}, s32[256]{0:T(256)}, u32[]{:S(2)}) copy-start(s32[256]{0:T(256)} %param.14) | copy-start | bytes 3076

commit v2 on v1

--- a/solution.py
+++ b/solution.py
@@ -97,18 +97,32 @@
     lax.fori_loop(0, block_len // 16, step, 0)
 
 
-def taps_of(ext, filter_ref, stream_id, i, ct, masks):
+def load_taps(filter_ref, stream_id, ct):
     cols = pl.ds(ct * LANES, LANES)
+    return [
+        jnp.broadcast_to(filter_ref[stream_id, shift : shift + 1, cols], (8, LANES)) for shift in range(3)
+    ]
+
+
+def filter_tile(ext, taps, i, ct, masks=None):
     pitch = ext.shape[0] // 8
     terms = []
     for shift in range(3):
-        tap = filter_ref[stream_id, shift : shift + 1, cols]
-        rows = pl.ds(ct * pitch + i * 8 + (8 - shift), 8)
-        term = tap * ext[rows, :]
+        term = taps[shift] * ext[pl.ds(ct * pitch + i * 8 + (8 - shift), 8), :]
         if shift and masks is not None:
             term = jnp.where(masks[shift - 1], term, 0.0)
         terms.append(term)
     return terms[0] + terms[1] + terms[2]
+
+
+def at_starts(firsts, first_pos, block_len, tile_len, redo):
+    for first in firsts:
+        for after in range(2):
+            place = first + after - first_pos
+
+            @pl.when((place >= 0) & (place < block_len))
+            def _():
+                redo(place // tile_len)
 
 
 def tile_masks(firsts, base):
@@ -138,28 +152,26 @@
     load_extended(ext_k, k_ref, edge_ref, 1)
     load_extended(ext_v, v_ref, edge_ref, 2)
 
-    def filter_step(i, _):
-        base = first_pos + i * 8
-
-        def fill(masks):
-            for ct in range(8):
-                k = taps_of(ext_k, filter_ref, 1, i, ct, masks)
-                v = taps_of(ext_v, filter_ref, 2, i, ct, masks)
-                driver[pl.ds(pl.multiple_of(i * 64 + ct * 8, 8), 8), :] = k * v
-
-        near = any_between(firsts, base - 1, base + 8)
-
-        @pl.when(near)
-        def _():
-            fill(tile_masks(firsts, base))
-
-        @pl.when(jnp.logical_not(near))
-        def _():
-            fill(None)
-
-        return 0
-
-    lax.fori_loop(0, block_len // 8, filter_step, 0)
+    for ct in range(8):
+        k_taps = load_taps(filter_ref, 1, ct)
+        v_taps = load_taps(filter_ref, 2, ct)
+
+        def filter_step(i, _):
+            k = filter_tile(ext_k, k_taps, i, ct)
+            v = filter_tile(ext_v, v_taps, i, ct)
+            driver[pl.ds(pl.multiple_of(i * 64 + ct * 8, 8), 8), :] = k * v
+            return 0
+
+        lax.fori_loop(0, block_len // 8, filter_step, 0, unroll=8)
+
+    def refilter(i):
+        masks = tile_masks(firsts, first_pos + i * 8)
+        for ct in range(8):
+            k = filter_tile(ext_k, load_taps(filter_ref, 1, ct), i, ct, masks)
+            v = filter_tile(ext_v, load_taps(filter_ref, 2, ct), i, ct, masks)
+            driver[pl.ds(pl.multiple_of(i * 64 + ct * 8, 8), 8), :] = k * v
+
+    at_starts(firsts, first_pos, block_len, 8, refilter)
 
     rates = to_sublanes(rate_ref, turn, poles)
     decays = [jnp.exp(-r) for r in rates]
@@ -237,34 +249,40 @@
         )
 
     in_ref[...] = jnp.zeros_like(in_ref)
-    for k in range(rounds):
+
+    def send(k, piece):
+        rows = pl.ds(piece * span, span)
+
+        @pl.when(me + (1 << k) < blocks)
+        def _():
+            whole = end_ref[rows, :]
+            if k:
+                fade = jnp.exp(-rate_ref[rows, :] * float(block_len)) * own_keep
+                whole = whole + fade * in_ref[rows, :]
+            outbox[k, rows, :] = whole.astype(jnp.bfloat16)
+            copy(k, piece).start()
+
+    def receive(k, piece):
+        rows = pl.ds(piece * span, span)
         reach = 1 << k
         far = first_pos - (reach - 1) * block_len
+
+        @pl.when(me >= reach)
+        def _():
+            copy(k, piece).wait_recv()
+            got = inbox[k, rows, :].astype(jnp.float32)
+            if k:
+                clear = jnp.where(last_start(first_pos - 1) < far, 1.0, 0.0)
+                got = got * (jnp.exp(-rate_ref[rows, :] * float((reach - 1) * block_len)) * clear)
+            in_ref[rows, :] += got
+
+    for piece in range(pieces):
+        send(0, piece)
+    for k in range(rounds):
         for piece in range(pieces):
-            rows = pl.ds(piece * span, span)
-
-            @pl.when(me + reach < blocks)
-            def _():
-                whole = end_ref[rows, :]
-                if k:
-                    fade = jnp.exp(-rate_ref[rows, :] * float(block_len)) * own_keep
-                    whole = whole + fade * in_ref[rows, :]
-                outbox[k, rows, :] = whole.astype(jnp.bfloat16)
-                copy(k, piece).start()
-
-        if k:
-            clear = jnp.where(last_start(first_pos - 1) < far, 1.0, 0.0)
-        for piece in range(pieces):
-            rows = pl.ds(piece * span, span)
-
-            @pl.when(me >= reach)
-            def _():
-                copy(k, piece).wait_recv()
-                got = inbox[k, rows, :].astype(jnp.float32)
-                if k:
-                    fade = jnp.exp(-rate_ref[rows, :] * float((reach - 1) * block_len))
-                    got = got * (fade * clear)
-                in_ref[rows, :] += got
+            receive(k, piece)
+            if k + 1 < rounds:
+                send(k + 1, piece)
 
     for k in range(rounds):
         for piece in range(pieces):
@@ -299,7 +317,7 @@
                 sums[p % 4] = sums[p % 4] + fading[p]
             arrived = (sums[0] + sums[1]) + (sums[2] + sums[3])
             rows = pl.ds(i * 64 + j, 8, stride=8)
-            y[rows, :] = y_in[0, rows, :] + jnp.where(i * 8 + j < cut, 1.0, 0.0) * arrived
+            y[rows, :] = jnp.where(i * 8 + j < cut, 1.0, 0.0) * arrived
             fading = [f * d for f, d in zip(fading, decays)]
         return tuple(fading)
 
@@ -308,38 +326,36 @@
 
     def plain_chunk(i, _):
         rows = pl.ds(pl.multiple_of(i * 64, 64), 64)
-        y[rows, :] = y_in[0, rows, :]
+        y[rows, :] = jnp.zeros((64, LANES), jnp.float32)
         return 0
 
     lax.fori_loop(carried, block_len // 8, plain_chunk, 0)
 
-    def gate_step(i, _):
-        base = first_pos + i * 16
-
-        def fill(masked):
-            for ct in range(8):
-                halves = []
-                for side in range(2):
-                    tile = i * 2 + side
-                    masks = tile_masks(firsts, base + side * 8) if masked else None
-                    q = taps_of(ext_q, filter_ref, 0, tile, ct, masks)
-                    halves.append(q * y[pl.ds(pl.multiple_of(tile * 64 + ct * 8, 8), 8), :])
-                both = jnp.concatenate(halves, axis=0).astype(jnp.bfloat16)
-                gated_ref[pl.ds(pl.multiple_of(i * 16, 16), 16), pl.ds(ct * LANES, LANES)] = both
-
-        near = any_between(firsts, base - 1, base + 16)
-
-        @pl.when(near)
-        def _():
-            fill(True)
-
-        @pl.when(jnp.logical_not(near))
-        def _():
-            fill(False)
-
-        return 0
-
-    lax.fori_loop(0, block_len // 16, gate_step, 0)
+    def gate(i, ct, taps, masks):
+        halves = []
+        for side in range(2):
+            tile = i * 2 + side
+            q = filter_tile(ext_q, taps, tile, ct, masks[side])
+            rows = pl.ds(pl.multiple_of(tile * 64 + ct * 8, 8), 8)
+            halves.append(q * (y_in[0, rows, :] + y[rows, :]))
+        both = jnp.concatenate(halves, axis=0).astype(jnp.bfloat16)
+        gated_ref[pl.ds(pl.multiple_of(i * 16, 16), 16), pl.ds(ct * LANES, LANES)] = both
+
+    for ct in range(8):
+        taps = load_taps(filter_ref, 0, ct)
+
+        def gate_step(i, _):
+            gate(i, ct, taps, [None, None])
+            return 0
+
+        lax.fori_loop(0, block_len // 16, gate_step, 0, unroll=4)
+
+    def regate(i):
+        masks = [tile_masks(firsts, first_pos + i * 16 + side * 8) for side in range(2)]
+        for ct in range(8):
+            gate(i, ct, load_taps(filter_ref, 0, ct), masks)
+
+    at_starts(firsts, first_pos, block_len, 16, regate)
     part = jnp.dot(gated_ref[...], unembed_ref[...], preferred_element_type=jnp.float32)
 
     @pl.when(group == 0)
@@ -453,7 +469,7 @@
 
     rounds = max(1, (blocks - 1).bit_length())
     rows = poles * groups * 8
-    pieces = 2
+    pieces = 4
     incoming = pl.pallas_call(
         functools.partial(exchange_kernel, blocks, block_len, pieces),
         name="exchange",

time: 63.5 us -> 58.2 us (0.917)
  Pallas kernels: 62 us -> 56.7 us
    pallas_call x1, Pallas kernels: 20.2 us -> 17.4 us  [local(): pl.pallas_call(local_kernel, name='recur', grid=(groups,), out_shape=[sha...]
    pallas_call x1, Pallas kernels: 19.8 us -> 18 us  [local(): pl.pallas_call(functools.partial(exchange_kernel, blocks, block_len, piec...]
where the time goes in v2:
time: 58.2 us; the launch traced here: 58.1 us
  Pallas kernels  56.7 us (97%)
  between operations  0.75 us (1%)
  local copies, waits for them, and re-layouts  0.59 us (1%)
    pallas_call x1, Pallas kernels, local(): pl.pallas_call(functools.partial(exchange_kernel, blocks, block_len, piec...  18 us
    pallas_call x1, Pallas kernels, local(): pl.pallas_call(local_kernel, name='recur', grid=(groups,), out_shape=[sha...  17.4 us
    pallas_call x1, Pallas kernels, local(): pl.pallas_call(finish_kernel, name='finish', grid=(groups,), out_shape=[s...  12.4 us
    pallas_call x1, Pallas kernels, local(): pl.pallas_call(functools.partial(edge_kernel, blocks), name='edges', grid...  5.16 us
    pallas_call x1, Pallas kernels, local(): pl.pallas_call(functools.partial(loss_kernel, parts), name='loss', out_sh...  3.73 us

profile of v2, /device:TPU:29, one launch (start us, length us, event | category | flops | bytes accessed | tf_op | source)
XLA Modules:
  0.0 58.1 jit_solution(14133156991912264727)
XLA Ops:
  0.6 0.0 copy-start.4
  0.6 0.0 copy-start
  0.7 0.0 copy-start.3
  0.7 0.0 copy-start.2
  0.7 0.0 copy-start.1
  0.7 5.2 %edges.1.edge_ref = f32[8,4096]{1,0:T(8,128)S(1)} custom-call(bf16[3,256,4096]{2,1,0:T(8,128)(2,1)} %q_ref.1), custom_call_target="tpu_custom_call" | custom-call | tf_op jit(solution)/shard_map/edges/pallas_call | solution.py:425
  5.9 0.0 copy-done.4
  5.9 0.0 copy-done
  5.9 0.0 copy-done.3
  5.9 0.0 copy-done.2
  5.9 0.0 copy-done.1
  5.9 17.4 %recur.1 = (f32[4,2048,128]{2,1,0:T(8,128)S(1)}, f32[16,4,8,128]{3,2,1,0:T(8,128)S(1)}, f32[16,4,8,128]{3,2,1,0:T(8,128)S(1)}, f32[16,4,8,128]{3,2,1,0:T(8,128)S(1)}) custom-call(s32[4]{0:T(128)S(1)} %copy-done.4, bf16[3,256,4096]{2,1,0:T(8,128)(2,1)} %q_ref.1, bf16[3,256,4096]{2,1,0:T(8,128)(2,1)} %q_ref.1, f32[8,4096]{1,0:T(8,128)S(1)} %edges.1.edge_ref, ...), custom_call_target="tpu_custom_call" | custom-call | tf_op jit(solution)/shard_map/recur/pallas_call | solution.py:451
  23.4 18.0 %exchange.1 = f32[512,128]{1,0:T(8,128)S(1)} custom-call(s32[4]{0:T(128)S(1)} %copy-done.4, f32[512,128]{1,0:T(8,128)S(1)} %bitcast.6, f32[512,128]{1,0:T(8,128)S(1)} %bitcast.8), custom_call_target="tpu_custom_call" | custom-call | tf_op jit(solution)/shard_map/exchange/pallas_call | solution.py:473
  41.4 0.0 copy-start.5
  41.4 12.4 %finish.1 = (bf16[256,4096]{1,0:T(8,128)(2,1)}, bf16[256,512]{1,0:T(8,128)(2,1)S(1)}) custom-call(s32[4]{0:T(128)S(1)} %copy-done.4, bf16[3,256,4096]{2,1,0:T(8,128)(2,1)} %q_ref.1, f32[8,4096]{1,0:T(8,128)S(1)} %edges.1.edge_ref, f32[3,3,4096]{2,1,0:T(4,128)S(1)} %copy-done, f32[16,4,8,128]{3,2,1,0:T(8,128)S(1)} %get-tuple-element.8.rate_ref, ...), custom_call_target="tpu_custom_call" | custom-call | tf_op jit(solution)/shard_map/finish/pallas_call | solution.py:488
  53.8 0.0 copy-done.5
  53.8 3.7 %loss.1 = f32[2,128]{1,0:T(2,128)S(1)} custom-call(bf16[256,512]{1,0:T(8,128)(2,1)S(1)} %get-tuple-element.13.logits_ref, s32[2,128]{1,0:T(2,128)S(1)} %bitcast.11), custom_call_target="tpu_custom_call" | custom-call | tf_op jit(solution)/shard_map/loss/pallas_call | solution.py:512
  57.5 0.6 copy.11
Async XLA Ops:
  0.6 5.2 %copy-start.4 = (s32[4]{0:T(128)S(1)}, s32[4]{0:T(128)}, u32[]{:S(2)}) copy-start(s32[4]{0:T(128)} %lengths_ref.5) | copy-start | bytes 52
  0.6 5.2 %copy-start = (f32[3,3,4096]{2,1,0:T(4,128)S(1)}, f32[3,3,4096]{2,1,0:T(4,128)}, u32[]{:S(2)}) copy-start(f32[3,3,4096]{2,1,0:T(4,128)} %filter_ref.3) | copy-start | bytes 442372
  0.7 5.2 %copy-start.3 = (f32[4096]{0:T(1024)S(1)}, f32[4096]{0:T(1024)}, u32[]{:S(2)}) copy-start(f32[4096]{0:T(1024)} %param.12) | copy-start | bytes 49156
  0.7 5.2 %copy-start.2 = (f32[16,4096]{1,0:T(8,128)S(1)}, f32[16,4096]{1,0:T(8,128)}, u32[]{:S(2)}) copy-start(f32[16,4096]{1,0:T(8,128)} %residue_ref.1) | copy-start | bytes 786436
  0.7 5.2 %copy-start.1 = (f32[16,4096]{1,0:T(8,128)S(1)}, f32[16,4096]{1,0:T(8,128)}, u32[]{:S(2)}) copy-start(f32[16,4096]{1,0:T(8,128)} %rate_ref.1) | copy-start | bytes 786436
  41.4 12.4 %copy-start.5 = (s32[256]{0:T(256)S(1)}, s32[256]{0:T(256)}, u32[]{:S(2)}) copy-start(s32[256]{0:T(256)} %param.14) | copy-start | bytes 3076

commit v3 on v2

v3 whole, which is shorter than its diff:
```python
import functools

import jax
import jax.numpy as jnp
from jax import lax
from jax.experimental import pallas as pl
from jax.experimental.pallas import tpu as pltpu
from jax.sharding import PartitionSpec as P

MESH = pl.DeviceIdType.MESH
LANES = 128
GROUP = 8 * LANES
VMEM_LIMIT = 48 * 1024 * 1024


def doc_firsts(lengths_ref):
    firsts = [jnp.int32(0)]
    for d in range(lengths_ref.shape[0] - 1):
        firsts.append(firsts[-1] + lengths_ref[d])
    return firsts


def any_between(firsts, low, high):
    found = jnp.bool_(False)
    for first in firsts:
        found = found | ((first >= low) & (first < high))
    return found


def greet(peers):
    barrier = pltpu.get_barrier_semaphore()
    for axis, peer, there in peers:

        @pl.when(there)
        def _():
            pl.semaphore_signal(barrier, inc=1, device_id={axis: peer}, device_id_type=MESH)

    if peers:
        pl.semaphore_wait(barrier, sum(jnp.where(there, 1, 0) for _, _, there in peers))


def load_edge(ext, edge_ref, stream_id, first_col=0):
    pitch = ext.shape[0] // 8
    for ct in range(8):
        edge = edge_ref[:, pl.ds(first_col + ct * LANES, LANES)]
        both = jnp.concatenate([edge[0:6], edge[2 * stream_id : 2 * stream_id + 2]], axis=0)
        ext[pl.ds(ct * pitch, 8), :] = both


def load_block(ext, stream_ref):
    block_len = stream_ref.shape[1]
    pitch = block_len + 8

    def step(i, _):
        rows = pl.ds(pl.multiple_of(i * 16, 16), 16)
        for ct in range(8):
            tile = stream_ref[0, rows, pl.ds(ct * LANES, LANES)].astype(jnp.float32)
            ext[pl.ds(pl.multiple_of(ct * pitch + i * 16 + 8, 8), 16), :] = tile
        return 0

    lax.fori_loop(0, block_len // 16, step, 0)


def load_taps(filter_ref, stream_id, ct):
    cols = pl.ds(ct * LANES, LANES)
    return [
        jnp.broadcast_to(filter_ref[stream_id, shift : shift + 1, cols], (8, LANES)) for shift in range(3)
    ]


def filter_tile(ext, taps, i, ct, masks=None):
    pitch = ext.shape[0] // 8
    terms = []
    for shift in range(3):
        term = taps[shift] * ext[pl.ds(ct * pitch + i * 8 + (8 - shift), 8), :]
        if shift and masks is not None:
            term = term * masks[shift - 1]
        terms.append(term)
    return terms[0] + terms[1] + terms[2]


def at_starts(firsts, first_pos, block_len, tile_len, redo):
    for first in firsts:
        for after in range(2):
            place = first + after - first_pos

            @pl.when((place >= 0) & (place < block_len))
            def _():
                redo(place // tile_len)


def tile_masks(firsts, base):
    pos = base + lax.broadcasted_iota(jnp.int32, (8, LANES), 0)
    start = jnp.zeros((8, LANES), jnp.int32)
    for first in firsts:
        start = jnp.maximum(start, jnp.where(first <= pos, first, 0))
    return [pos - shift >= start for shift in (1, 2)]


def to_sublanes(ref, scratch, row_count):
    for top in range(0, row_count, 8):
        for ct in range(8):
            scratch[pl.ds(top * 8 + ct * 8, 8), :] = ref[top : top + 8, pl.ds(ct * LANES, LANES)]
    return [scratch[pl.ds((p // 8) * 64 + p % 8, 8, stride=8), :] for p in range(row_count)]


def recur_kernel(
    blocks, groups,
    lengths_ref, tail_ref, k_ref, v_ref, filter_ref, rate_ref, residue_ref, direct_ref,
    y_ref, edge_ref, rate_out, weight_out, in_ref,
    ext_k, ext_v, turn, driver, mask_1, mask_2, table, ends,
    packed, landed, outbox, inbox, edge_send, edge_recv, send_sem, recv_sem,
):
    block_len = k_ref.shape[1]
    poles = rate_ref.shape[0]
    span = poles * 8
    group = pl.program_id(0)
    me = lax.axis_index("seq")
    first_pos = me * block_len
    firsts = doc_firsts(lengths_ref)
    rounds = max(1, (blocks - 1).bit_length())
    half = packed.shape[1]

    def last_start(pos):
        best = jnp.int32(0)
        for first in firsts:
            best = jnp.maximum(best, jnp.where(first <= pos, first, 0))
        return best

    edge_copy = pltpu.make_async_remote_copy(
        src_ref=packed,
        dst_ref=landed,
        send_sem=edge_send,
        recv_sem=edge_recv,
        device_id={"seq": me + 1},
        device_id_type=MESH,
    )

    def state_copy(k, piece):
        rows = pl.ds(pl.multiple_of(piece * span, span), span)
        return pltpu.make_async_remote_copy(
            src_ref=outbox.at[k, rows],
            dst_ref=inbox.at[k, rows],
            send_sem=send_sem.at[k, piece],
            recv_sem=recv_sem.at[k, piece],
            device_id={"seq": me + (1 << k)},
            device_id_type=MESH,
        )

    own_keep = jnp.where(last_start(first_pos + block_len - 1) < first_pos, 1.0, 0.0)

    def send(k, piece):
        rows = pl.ds(pl.multiple_of(piece * span, span), span)

        @pl.when(me + (1 << k) < blocks)
        def _():
            whole = ends[rows, :]
            if k:
                fade = jnp.exp(-rate_out[rows, :] * float(block_len)) * own_keep
                whole = whole + fade * in_ref[rows, :]
            outbox[k, rows, :] = whole.astype(jnp.bfloat16)
            state_copy(k, piece).start()

    def receive(k, piece):
        rows = pl.ds(pl.multiple_of(piece * span, span), span)
        reach = 1 << k
        far = first_pos - (reach - 1) * block_len

        @pl.when(me >= reach)
        def _():
            state_copy(k, piece).wait_recv()
            got = inbox[k, rows, :].astype(jnp.float32)
            if k:
                clear = jnp.where(last_start(first_pos - 1) < far, 1.0, 0.0)
                got = got * (jnp.exp(-rate_out[rows, :] * float((reach - 1) * block_len)) * clear)
            in_ref[rows, :] += got

    def relay(k, piece):
        receive(k, piece)
        if k + 1 < rounds:
            send(k + 1, piece)

    @pl.when(group == 0)
    def _():
        rows = []
        for side in range(2):
            cols = pl.ds(side * half, half)
            for j in range(3):
                rows.append(tail_ref[j, :, cols].astype(jnp.float32)[14:16])
            rows.append(jnp.zeros((2, half), jnp.float32))
        packed[...] = jnp.concatenate(rows, axis=0).astype(jnp.bfloat16)
        peers = []
        for k in range(rounds):
            peers.append(("seq", me + (1 << k), me + (1 << k) < blocks))
            peers.append(("seq", me - (1 << k), me >= (1 << k)))
        greet(peers)

        @pl.when(me < blocks - 1)
        def _():
            edge_copy.start()

        in_ref[...] = jnp.zeros_like(in_ref)
        table[pl.ds(span, span), :] = jnp.zeros((span, LANES), jnp.float32)
        for i in range(block_len // 8):
            masks = tile_masks(firsts, first_pos + i * 8)
            mask_1[pl.ds(i * 8, 8), :] = jnp.where(masks[0], 1.0, 0.0)
            mask_2[pl.ds(i * 8, 8), :] = jnp.where(masks[1], 1.0, 0.0)

    load_block(ext_k, k_ref)
    load_block(ext_v, v_ref)

    rates = to_sublanes(rate_ref, turn, poles)
    decays = [jnp.exp(-r) for r in rates]
    own = pl.multiple_of(group * span, span)
    for p in range(poles):
        rate_out[pl.ds(own + p * 8, 8), :] = rates[p]
        table[pl.ds(p * 8, 8), :] = decays[p]
    residues = to_sublanes(residue_ref, turn, poles)
    weights = [residues[p] * (1.0 - decays[p]) for p in range(poles)]
    for p in range(poles):
        weight_out[pl.ds(own + p * 8, 8), :] = weights[p]
    for ct in range(8):
        turn[pl.ds(ct * 8, 8), :] = jnp.broadcast_to(direct_ref[:, pl.ds(ct * LANES, LANES)], (8, LANES))
    direct = turn[pl.ds(0, 8, stride=8), :]

    @pl.when(group == 0)
    def _():
        @pl.when(me > 0)
        def _():
            edge_copy.wait_recv()
            got = landed[...].astype(jnp.float32)
            edge_ref[:, pl.ds(0, half)] = got[0:8]
            edge_ref[:, pl.ds(half, half)] = got[8:16]

        @pl.when(me == 0)
        def _():
            edge_ref[...] = jnp.zeros_like(edge_ref)

    first_col = pl.multiple_of(group * GROUP, GROUP)
    load_edge(ext_k, edge_ref, 1, first_col)
    load_edge(ext_v, edge_ref, 2, first_col)

    for ct in range(8):
        k_taps = load_taps(filter_ref, 1, ct)
        v_taps = load_taps(filter_ref, 2, ct)

        def filter_step(i, _):
            rows = pl.ds(pl.multiple_of(i * 8, 8), 8)
            masks = (mask_1[rows, :], mask_2[rows, :])
            k = filter_tile(ext_k, k_taps, i, ct, masks)
            v = filter_tile(ext_v, v_taps, i, ct, masks)
            driver[pl.ds(pl.multiple_of(i * 64 + ct * 8, 8), 8), :] = k * v
            return 0

        lax.fori_loop(0, block_len // 8, filter_step, 0, unroll=8)

    def chunk(i, states):
        states = list(states)
        for j in range(8):
            x = driver[pl.ds(i * 64 + j, 8, stride=8), :]
            place = first_pos + i * 8 + j
            bank = jnp.where(any_between(firsts, place, place + 1), span, 0)
            sums = [direct * x, None, None, None]
            for p in range(poles):
                states[p] = table[pl.ds(bank + p * 8, 8), :] * states[p] + x
                term = weights[p] * states[p]
                sums[p % 4] = term if sums[p % 4] is None else sums[p % 4] + term
            y_ref[0, pl.ds(i * 64 + j, 8, stride=8), :] = (sums[0] + sums[1]) + (sums[2] + sums[3])
        return tuple(states)

    chunks = block_len // 8
    states = tuple(jnp.zeros((8, LANES), jnp.float32) for _ in range(poles))
    states = lax.fori_loop(0, chunks // 2, chunk, states)
    for k in range(0, rounds, 2):
        piece = group - 1 - k // 2

        @pl.when(piece >= 0)
        def _():
            relay(k, piece)

    states = lax.fori_loop(chunks // 2, chunks, chunk, states)
    for p in range(poles):
        ends[pl.ds(own + p * 8, 8), :] = states[p]
    send(0, group)
    for k in range(1, rounds, 2):
        piece = group - (k + 1) // 2

        @pl.when(piece >= 0)
        def _():
            relay(k, piece)

    @pl.when(group == groups - 1)
    def _():
        for slot in range(2 * groups, 2 * groups + rounds):
            for k in reversed(range(rounds)):
                piece, odd = divmod(slot - 2 - k, 2)
                if odd == 0 and 0 <= piece < groups:
                    relay(k, piece)
        for k in range(rounds):
            for piece in range(groups):

                @pl.when(me + (1 << k) < blocks)
                def _():
                    state_copy(k, piece).wait_send()

        @pl.when(me < blocks - 1)
        def _():
            edge_copy.wait_send()


def finish_kernel(
    lengths_ref, q_ref, edge_ref, filter_ref, rate_ref, weight_ref, in_ref, y_in, unembed_ref,
    gated_ref, logits_ref,
    ext_q, y, total,
):
    block_len = q_ref.shape[1]
    poles = rate_ref.shape[0] // 8
    first_pos = lax.axis_index("seq") * block_len
    firsts = doc_firsts(lengths_ref)
    group = pl.program_id(0)
    cut = jnp.int32(block_len)
    for first in firsts:
        cut = jnp.where(first >= first_pos, jnp.minimum(cut, first - first_pos), cut)
    load_block(ext_q, q_ref)
    load_edge(ext_q, edge_ref, 0)
    tiles = [pl.ds(p * 8, 8) for p in range(poles)]
    decays = [jnp.exp(-rate_ref[tile, :]) for tile in tiles]
    fading = tuple(weight_ref[tile, :] * in_ref[tile, :] * d for tile, d in zip(tiles, decays))

    def fade_chunk(i, fading):
        fading = list(fading)
        for j in range(8):
            sums = [fading[0], fading[1], fading[2], fading[3]]
            for p in range(4, poles):
                sums[p % 4] = sums[p % 4] + fading[p]
            arrived = (sums[0] + sums[1]) + (sums[2] + sums[3])
            rows = pl.ds(i * 64 + j, 8, stride=8)
            y[rows, :] = jnp.where(i * 8 + j < cut, 1.0, 0.0) * arrived
            fading = [f * d for f, d in zip(fading, decays)]
        return tuple(fading)

    carried = (cut + 7) // 8
    lax.fori_loop(0, carried, fade_chunk, fading)

    def plain_chunk(i, _):
        rows = pl.ds(pl.multiple_of(i * 64, 64), 64)
        y[rows, :] = jnp.zeros((64, LANES), jnp.float32)
        return 0

    lax.fori_loop(carried, block_len // 8, plain_chunk, 0)

    def gate(i, ct, taps, masks):
        halves = []
        for side in range(2):
            tile = i * 2 + side
            q = filter_tile(ext_q, taps, tile, ct, masks[side])
            rows = pl.ds(pl.multiple_of(tile * 64 + ct * 8, 8), 8)
            halves.append(q * (y_in[0, rows, :] + y[rows, :]))
        both = jnp.concatenate(halves, axis=0).astype(jnp.bfloat16)
        gated_ref[pl.ds(pl.multiple_of(i * 16, 16), 16), pl.ds(ct * LANES, LANES)] = both

    for ct in range(8):
        taps = load_taps(filter_ref, 0, ct)

        def gate_step(i, _):
            gate(i, ct, taps, [None, None])
            return 0

        lax.fori_loop(0, block_len // 16, gate_step, 0, unroll=4)

    def regate(i):
        masks = []
        for side in range(2):
            pair = tile_masks(firsts, first_pos + i * 16 + side * 8)
            masks.append([jnp.where(m, 1.0, 0.0) for m in pair])
        for ct in range(8):
            gate(i, ct, load_taps(filter_ref, 0, ct), masks)

    at_starts(firsts, first_pos, block_len, 16, regate)
    part = jnp.dot(gated_ref[...], unembed_ref[...], preferred_element_type=jnp.float32)

    @pl.when(group == 0)
    def _():
        total[...] = part

    @pl.when(group > 0)
    def _():
        total[...] += part

    @pl.when(group == pl.num_programs(0) - 1)
    def _():
        logits_ref[...] = total[...].astype(jnp.bfloat16)


def loss_kernel(parts, logits_ref, target_ref, loss_ref, inbox, send_sem, recv_sem):
    me = lax.axis_index("chan")
    others = [lax.rem(me + d, parts) for d in range(1, parts)]
    greet([("chan", other, me >= 0) for other in others])
    copies = []
    for d in range(1, parts):
        copies.append(
            pltpu.make_async_remote_copy(
                src_ref=logits_ref,
                dst_ref=inbox.at[me],
                send_sem=send_sem.at[d - 1],
                recv_sem=recv_sem.at[d - 1],
                device_id={"chan": others[d - 1]},
                device_id_type=MESH,
            )
        )
        copies[-1].start()
    inbox[me] = logits_ref[...]
    for copy in copies:
        copy.wait_recv()
    block_len, vocab = logits_ref.shape
    eye = lax.broadcasted_iota(jnp.int32, (LANES, LANES), 0) == lax.broadcasted_iota(
        jnp.int32, (LANES, LANES), 1
    )
    vocab_ids = lax.broadcasted_iota(jnp.int32, (LANES, vocab), 1)
    for tile in range(block_len // LANES):
        rows = pl.ds(tile * LANES, LANES)
        logits = inbox[0, rows, :].astype(jnp.float32)
        for part in range(1, parts):
            logits = logits + inbox[part, rows, :].astype(jnp.float32)
        wanted = jnp.where(eye, target_ref[tile : tile + 1, :].astype(jnp.float32), 0.0)
        wanted = jnp.sum(wanted, axis=1, keepdims=True).astype(jnp.int32)
        peak = jnp.max(logits, axis=1, keepdims=True)
        exp_total = jnp.sum(jnp.exp(logits - peak), axis=1, keepdims=True)
        picked = jnp.sum(jnp.where(vocab_ids == wanted, logits, 0.0), axis=1, keepdims=True)
        loss = peak + jnp.log(exp_total) - picked
        loss_ref[tile : tile + 1, :] = jnp.sum(jnp.where(eye, loss, 0.0), axis=0, keepdims=True)
    for copy in copies:
        copy.wait_send()


def local(blocks, parts, streams, short_filter, pole_rates, residues, direct, doc_lengths, targets, unembed):
    block_len, chans = streams.shape[1], streams.shape[2]
    poles, vocab = pole_rates.shape[0], unembed.shape[1]
    groups = chans // GROUP
    f32, bf16 = jnp.float32, jnp.bfloat16
    shape = jax.ShapeDtypeStruct
    vmem = pl.BlockSpec(memory_space=pltpu.VMEM)
    smem = pl.BlockSpec(memory_space=pltpu.SMEM)
    params = functools.partial(pltpu.CompilerParams, vmem_limit_bytes=VMEM_LIMIT)

    def stream_spec(j):
        return pl.BlockSpec((1, block_len, GROUP), lambda g: (j, 0, g))

    rounds = max(1, (blocks - 1).bit_length())
    rows = poles * groups * 8
    filter_spec = pl.BlockSpec((3, 3, GROUP), lambda g: (0, 0, g))
    pole_spec = pl.BlockSpec((poles, GROUP), lambda g: (0, g))
    rows_spec = pl.BlockSpec((rows, LANES), lambda g: (0, 0))
    y_spec = pl.BlockSpec((1, block_len * 8, LANES), lambda g: (g, 0, 0))

    y_local, edges, rates, weights, incoming = pl.pallas_call(
        functools.partial(recur_kernel, blocks, groups),
        name="recur",
        grid=(groups,),
        out_shape=[
            shape((groups, block_len * 8, LANES), f32),
            shape((8, chans), f32),
            shape((rows, LANES), f32),
            shape((rows, LANES), f32),
            shape((rows, LANES), f32),
        ],
        in_specs=[
            smem,
            pl.BlockSpec((3, 16, chans), lambda g: (0, block_len // 16 - 1, 0)),
            stream_spec(1), stream_spec(2), filter_spec, pole_spec, pole_spec,
            pl.BlockSpec((1, GROUP), lambda g: (0, g)),
        ],
        out_specs=[y_spec, pl.BlockSpec((8, chans), lambda g: (0, 0)), rows_spec, rows_spec, rows_spec],
        scratch_shapes=[
            pltpu.VMEM((8 * (block_len + 8), LANES), f32),
            pltpu.VMEM((8 * (block_len + 8), LANES), f32),
            pltpu.VMEM((poles * 8, LANES), f32),
            pltpu.VMEM((block_len * 8, LANES), f32),
            pltpu.VMEM((block_len, LANES), f32),
            pltpu.VMEM((block_len, LANES), f32),
            pltpu.VMEM((2 * poles * 8, LANES), f32),
            pltpu.VMEM((rows, LANES), f32),
            pltpu.VMEM((16, chans // 2), bf16),
            pltpu.VMEM((16, chans // 2), bf16),
            pltpu.VMEM((rounds, rows, LANES), bf16),
            pltpu.VMEM((rounds, rows, LANES), bf16),
            pltpu.SemaphoreType.DMA,
            pltpu.SemaphoreType.DMA,
            pltpu.SemaphoreType.DMA((rounds, groups)),
            pltpu.SemaphoreType.DMA((rounds, groups)),
        ],
        compiler_params=params(collective_id=0, has_side_effects=True),
    )(doc_lengths, streams, streams, streams, short_filter, pole_rates, residues, direct.reshape(1, chans))

    turned_spec = pl.BlockSpec((poles * 8, LANES), lambda g: (g, 0))
    edge_spec = pl.BlockSpec((8, GROUP), lambda g: (0, g))
    gated_out, logits = pl.pallas_call(
        finish_kernel,
        name="finish",
        grid=(groups,),
        out_shape=[shape((block_len, chans), bf16), shape((block_len, vocab), bf16)],
        in_specs=[
            smem, stream_spec(0), edge_spec, filter_spec, turned_spec, turned_spec, turned_spec, y_spec,
            pl.BlockSpec((GROUP, vocab), lambda g: (g, 0)),
        ],
        out_specs=[
            pl.BlockSpec((block_len, GROUP), lambda g: (0, g)),
            pl.BlockSpec((block_len, vocab), lambda g: (0, 0)),
        ],
        scratch_shapes=[
            pltpu.VMEM((8 * (block_len + 8), LANES), f32),
            pltpu.VMEM((block_len * 8, LANES), f32),
            pltpu.VMEM((block_len, vocab), f32),
        ],
        compiler_params=params(),
    )(
        doc_lengths, streams, edges, short_filter, rates, weights,
        incoming, y_local, unembed,
    )

    loss = pl.pallas_call(
        functools.partial(loss_kernel, parts),
        name="loss",
        out_shape=shape((block_len // LANES, LANES), f32),
        in_specs=[vmem, vmem],
        out_specs=vmem,
        scratch_shapes=[
            pltpu.VMEM((parts, block_len, vocab), bf16),
            pltpu.SemaphoreType.DMA((max(1, parts - 1),)),
            pltpu.SemaphoreType.DMA((max(1, parts - 1),)),
        ],
        compiler_params=params(collective_id=1, has_side_effects=True),
    )(logits, targets.reshape(block_len // LANES, LANES))
    return gated_out, loss.reshape(block_len)


def solution(mesh):
    in_specs = (
        P(None, "seq", "chan"),
        P(None, None, "chan"),
        P(None, "chan"),
        P(None, "chan"),
        P("chan"),
        P(),
        P("seq"),
        P("chan", None),
    )
    out_specs = (P("seq", "chan"), P("seq"))
    body = functools.partial(local, mesh.shape["seq"], mesh.shape["chan"])
    return jax.shard_map(body, mesh=mesh, in_specs=in_specs, out_specs=out_specs, check_vma=False)
```

time: 58.2 us -> 56.4 us (0.969)
  Pallas kernels: 56.7 us -> 50.6 us
  local copies, waits for them, and re-layouts: 0.59 us -> 4.76 us
    pallas_call x3 -> x1, Pallas kernels: 40.6 us -> 31.4 us  [local(): pl.pallas_call(functools.partial(recur_kernel, blocks, groups), name='rec...]
    unnamed x13, local copies, waits for them, and re-layouts: 0.59 us -> 4.76 us
    pallas_call x1, Pallas kernels: 3.73 us -> 6.9 us  [local(): pl.pallas_call(functools.partial(loss_kernel, parts), name='loss', out_sh...]
where the time goes in v3:
time: 56.4 us; the launch traced here: 56 us
  Pallas kernels  50.6 us (90%)
  local copies, waits for them, and re-layouts  4.76 us (8%)
  between operations  0.67 us (1%)
    pallas_call x1, Pallas kernels, local(): pl.pallas_call(functools.partial(recur_kernel, blocks, groups), name='rec...  31.4 us
    pallas_call x1, Pallas kernels, local(): pl.pallas_call(finish_kernel, name='finish', grid=(groups,), out_shape=[s...  12.3 us
    pallas_call x1, Pallas kernels, local(): pl.pallas_call(functools.partial(loss_kernel, parts), name='loss', out_sh...  6.9 us
    unnamed x13, local copies, waits for them, and re-layouts  4.76 us

profile of v3, /device:TPU:29, one launch (start us, length us, event | category | flops | bytes accessed | tf_op | source)
XLA Modules:
  0.0 56.0 jit_solution(11668275971967334054)
XLA Ops:
  0.6 0.0 copy-start
  0.6 0.9 %copy-done = f32[3,3,4096]{2,1,0:T(4,128)S(1)} copy-done((f32[3,3,4096]{2,1,0:T(4,128)S(1)}, f32[3,3,4096]{2,1,0:T(4,128)}, u32[]{:S(2)}) %copy-start) | copy-done | bytes 147480
  1.6 0.0 copy-start.1
  1.6 0.9 %copy-done.1 = f32[16,4096]{1,0:T(8,128)S(1)} copy-done((f32[16,4096]{1,0:T(8,128)S(1)}, f32[16,4096]{1,0:T(8,128)}, u32[]{:S(2)}) %copy-start.1) | copy-done | bytes 262168
  2.5 0.0 copy-start.2
  2.5 0.9 %copy-done.2 = f32[16,4096]{1,0:T(8,128)S(1)} copy-done((f32[16,4096]{1,0:T(8,128)S(1)}, f32[16,4096]{1,0:T(8,128)}, u32[]{:S(2)}) %copy-start.2) | copy-done | bytes 262168
  3.5 0.0 copy-start.3
  3.5 0.7 %copy-done.3 = f32[4096]{0:T(1024)S(1)} copy-done((f32[4096]{0:T(1024)S(1)}, f32[4096]{0:T(1024)}, u32[]{:S(2)}) %copy-start.3) | copy-done | bytes 16408
  4.2 0.0 copy-start.4
  4.2 0.7 %copy-done.4 = s32[4]{0:T(128)S(1)} copy-done((s32[4]{0:T(128)S(1)}, s32[4]{0:T(128)}, u32[]{:S(2)}) %copy-start.4) | copy-done | bytes 40
  4.8 31.4 %recur.1 = (f32[4,2048,128]{2,1,0:T(8,128)S(1)}, f32[8,4096]{1,0:T(8,128)S(1)}, f32[512,128]{1,0:T(8,128)S(1)}, f32[512,128]{1,0:T(8,128)S(1)}, f32[512,128]{1,0:T(8,128)S(1)}) custom-call(s32[4]{0:T(128)S(1)} %copy-done.4, bf16[3,256,4096]{2,1,0:T(8,128)(2,1)} %q_ref.1, bf16[3,256,4096]{2,1,0:T(8,128)(2,1)} %q_ref.1, bf16[3,256,4096]{2,1,0:T(8,128)(2,1)} %q_ref.1, ...), custom_call_target="tpu_custom_call" | custom-call | tf_op jit(solution)/shard_map/recur/pallas_call | solution.py:456
  36.2 0.0 copy-start.5
  36.2 12.3 %finish.1 = (bf16[256,4096]{1,0:T(8,128)(2,1)}, bf16[256,512]{1,0:T(8,128)(2,1)S(1)}) custom-call(s32[4]{0:T(128)S(1)} %copy-done.4, bf16[3,256,4096]{2,1,0:T(8,128)(2,1)} %q_ref.1, f32[8,4096]{1,0:T(8,128)S(1)} %get-tuple-element.9.edge_ref, f32[3,3,4096]{2,1,0:T(4,128)S(1)} %copy-done, f32[512,128]{1,0:T(8,128)S(1)} %get-tuple-element.10.rate_ref, ...), custom_call_target="tpu_custom_call" | custom-call | tf_op jit(solution)/shard_map/finish/pallas_call | solution.py:497
  48.5 0.0 copy-done.5
  48.5 6.9 %loss.1 = f32[2,128]{1,0:T(2,128)S(1)} custom-call(bf16[256,512]{1,0:T(8,128)(2,1)S(1)} %get-tuple-element.15.logits_ref, s32[2,128]{1,0:T(2,128)S(1)} %bitcast.5), custom_call_target="tpu_custom_call" | custom-call | tf_op jit(solution)/shard_map/loss/pallas_call | solution.py:521
  55.4 0.6 %copy.11 = f32[256]{0:T(256)} copy(f32[256]{0:T(256)S(1)} %bitcast.4) | data formatting | bytes 2048
Async XLA Ops:
  0.6 0.9 %copy-start = (f32[3,3,4096]{2,1,0:T(4,128)S(1)}, f32[3,3,4096]{2,1,0:T(4,128)}, u32[]{:S(2)}) copy-start(f32[3,3,4096]{2,1,0:T(4,128)} %filter_ref.3) | copy-start | bytes 442372
  1.6 0.9 %copy-start.1 = (f32[16,4096]{1,0:T(8,128)S(1)}, f32[16,4096]{1,0:T(8,128)}, u32[]{:S(2)}) copy-start(f32[16,4096]{1,0:T(8,128)} %rate_ref.1) | copy-start | bytes 786436
  2.5 0.9 %copy-start.2 = (f32[16,4096]{1,0:T(8,128)S(1)}, f32[16,4096]{1,0:T(8,128)}, u32[]{:S(2)}) copy-start(f32[16,4096]{1,0:T(8,128)} %residue_ref.1) | copy-start | bytes 786436
  3.5 0.7 %copy-start.3 = (f32[4096]{0:T(1024)S(1)}, f32[4096]{0:T(1024)}, u32[]{:S(2)}) copy-start(f32[4096]{0:T(1024)} %param.12) | copy-start | bytes 49156
  4.2 0.7 %copy-start.4 = (s32[4]{0:T(128)S(1)}, s32[4]{0:T(128)}, u32[]{:S(2)}) copy-start(s32[4]{0:T(128)} %lengths_ref.3) | copy-start | bytes 52
  36.2 12.3 %copy-start.5 = (s32[256]{0:T(256)S(1)}, s32[256]{0:T(256)}, u32[]{:S(2)}) copy-start(s32[256]{0:T(256)} %param.14) | copy-start | bytes 3076

commit v4 on v3

--- a/solution.py
+++ b/solution.py
@@ -10,7 +10,7 @@
 MESH = pl.DeviceIdType.MESH
 LANES = 128
 GROUP = 8 * LANES
-VMEM_LIMIT = 48 * 1024 * 1024
+VMEM_LIMIT = 65200 * 1024
 
 
 def doc_firsts(lengths_ref):
@@ -39,68 +39,44 @@
         pl.semaphore_wait(barrier, sum(jnp.where(there, 1, 0) for _, _, there in peers))
 
 
-def load_edge(ext, edge_ref, stream_id, first_col=0):
-    pitch = ext.shape[0] // 8
-    for ct in range(8):
-        edge = edge_ref[:, pl.ds(first_col + ct * LANES, LANES)]
-        both = jnp.concatenate([edge[0:6], edge[2 * stream_id : 2 * stream_id + 2]], axis=0)
-        ext[pl.ds(ct * pitch, 8), :] = both
-
-
-def load_block(ext, stream_ref):
+def load_block(raw, stream_ref):
     block_len = stream_ref.shape[1]
-    pitch = block_len + 8
 
     def step(i, _):
         rows = pl.ds(pl.multiple_of(i * 16, 16), 16)
         for ct in range(8):
             tile = stream_ref[0, rows, pl.ds(ct * LANES, LANES)].astype(jnp.float32)
-            ext[pl.ds(pl.multiple_of(ct * pitch + i * 16 + 8, 8), 16), :] = tile
+            raw[pl.ds(pl.multiple_of(i * 128 + ct * 8, 8), 8), :] = tile[0:8]
+            raw[pl.ds(pl.multiple_of(i * 128 + 64 + ct * 8, 8), 8), :] = tile[8:16]
         return 0
 
-    lax.fori_loop(0, block_len // 16, step, 0)
-
-
-def load_taps(filter_ref, stream_id, ct):
-    cols = pl.ds(ct * LANES, LANES)
-    return [
-        jnp.broadcast_to(filter_ref[stream_id, shift : shift + 1, cols], (8, LANES)) for shift in range(3)
-    ]
-
-
-def filter_tile(ext, taps, i, ct, masks=None):
-    pitch = ext.shape[0] // 8
-    terms = []
-    for shift in range(3):
-        term = taps[shift] * ext[pl.ds(ct * pitch + i * 8 + (8 - shift), 8), :]
-        if shift and masks is not None:
-            term = term * masks[shift - 1]
-        terms.append(term)
-    return terms[0] + terms[1] + terms[2]
-
-
-def at_starts(firsts, first_pos, block_len, tile_len, redo):
-    for first in firsts:
-        for after in range(2):
-            place = first + after - first_pos
-
-            @pl.when((place >= 0) & (place < block_len))
-            def _():
-                redo(place // tile_len)
-
-
-def tile_masks(firsts, base):
-    pos = base + lax.broadcasted_iota(jnp.int32, (8, LANES), 0)
-    start = jnp.zeros((8, LANES), jnp.int32)
-    for first in firsts:
-        start = jnp.maximum(start, jnp.where(first <= pos, first, 0))
-    return [pos - shift >= start for shift in (1, 2)]
-
-
-def to_sublanes(ref, scratch, row_count):
+    lax.fori_loop(0, block_len // 16, step, 0, unroll=2)
+
+
+def load_taps(filter_ref, turn, stream_id, bank_table, slot):
+    for ct in range(8):
+        turn[pl.ds(ct * 8, 3), :] = filter_ref[stream_id, :, pl.ds(ct * LANES, LANES)]
+    taps = [turn[pl.ds(shift, 8, stride=8), :] for shift in range(3)]
+    width = bank_table.shape[0] // 3
+    zero = jnp.zeros((8, LANES), jnp.float32)
+    for bank, pair in enumerate(((taps[1], taps[2]), (zero, zero), (taps[1], zero))):
+        for n in range(2):
+            bank_table[pl.ds(bank * width + (slot * 2 + n) * 8, 8), :] = pair[n]
+    return taps[0]
+
+
+def filtered_token(tap, bank_table, bank_row, slot, now, back_1, back_2):
+    tap_1 = bank_table[pl.ds(bank_row + slot * 16, 8), :]
+    tap_2 = bank_table[pl.ds(bank_row + slot * 16 + 8, 8), :]
+    return tap * now + tap_1 * back_1 + tap_2 * back_2
+
+
+def to_sublanes(ref, scratch, row_count, first_col=0):
     for top in range(0, row_count, 8):
         for ct in range(8):
-            scratch[pl.ds(top * 8 + ct * 8, 8), :] = ref[top : top + 8, pl.ds(ct * LANES, LANES)]
+            scratch[pl.ds(top * 8 + ct * 8, 8), :] = ref[
+                top : top + 8, pl.ds(first_col + ct * LANES, LANES)
+            ]
     return [scratch[pl.ds((p // 8) * 64 + p % 8, 8, stride=8), :] for p in range(row_count)]
 
 
@@ -108,7 +84,7 @@
     blocks, groups,
     lengths_ref, tail_ref, k_ref, v_ref, filter_ref, rate_ref, residue_ref, direct_ref,
     y_ref, edge_ref, rate_out, weight_out, in_ref,
-    ext_k, ext_v, turn, driver, mask_1, mask_2, table, ends,
+    raw_k, raw_v, turn, table, tap_table, ends,
     packed, landed, outbox, inbox, edge_send, edge_recv, send_sem, recv_sem,
 ):
     block_len = k_ref.shape[1]
@@ -201,13 +177,9 @@
 
         in_ref[...] = jnp.zeros_like(in_ref)
         table[pl.ds(span, span), :] = jnp.zeros((span, LANES), jnp.float32)
-        for i in range(block_len // 8):
-            masks = tile_masks(firsts, first_pos + i * 8)
-            mask_1[pl.ds(i * 8, 8), :] = jnp.where(masks[0], 1.0, 0.0)
-            mask_2[pl.ds(i * 8, 8), :] = jnp.where(masks[1], 1.0, 0.0)
-
-    load_block(ext_k, k_ref)
-    load_block(ext_v, v_ref)
+
+    load_block(raw_k, k_ref)
+    load_block(raw_v, v_ref)
 
     rates = to_sublanes(rate_ref, turn, poles)
     decays = [jnp.exp(-r) for r in rates]
@@ -236,40 +208,36 @@
         def _():
             edge_ref[...] = jnp.zeros_like(edge_ref)
 
-    first_col = pl.multiple_of(group * GROUP, GROUP)
-    load_edge(ext_k, edge_ref, 1, first_col)
-    load_edge(ext_v, edge_ref, 2, first_col)
-
-    for ct in range(8):
-        k_taps = load_taps(filter_ref, 1, ct)
-        v_taps = load_taps(filter_ref, 2, ct)
-
-        def filter_step(i, _):
-            rows = pl.ds(pl.multiple_of(i * 8, 8), 8)
-            masks = (mask_1[rows, :], mask_2[rows, :])
-            k = filter_tile(ext_k, k_taps, i, ct, masks)
-            v = filter_tile(ext_v, v_taps, i, ct, masks)
-            driver[pl.ds(pl.multiple_of(i * 64 + ct * 8, 8), 8), :] = k * v
-            return 0
-
-        lax.fori_loop(0, block_len // 8, filter_step, 0, unroll=8)
-
-    def chunk(i, states):
-        states = list(states)
+    edges = to_sublanes(edge_ref, turn, 8, pl.multiple_of(group * GROUP, GROUP))
+    k_tap = load_taps(filter_ref, turn, 1, tap_table, 0)
+    v_tap = load_taps(filter_ref, turn, 2, tap_table, 1)
+
+    def chunk(i, carry):
+        states, (k_1, k_2, v_1, v_2) = list(carry[:poles]), carry[poles:]
+        place = first_pos + i * 8
+        after = any_between(firsts, place - 1, place)
         for j in range(8):
-            x = driver[pl.ds(i * 64 + j, 8, stride=8), :]
-            place = first_pos + i * 8 + j
-            bank = jnp.where(any_between(firsts, place, place + 1), span, 0)
+            rows = pl.ds(i * 64 + j, 8, stride=8)
+            starts = any_between(firsts, place + j, place + j + 1)
+            bank = jnp.where(starts, span, 0)
+            tap_row = jnp.where(starts, 32, jnp.where(after, 64, 0))
+            after = starts
+            k_0, v_0 = raw_k[rows, :], raw_v[rows, :]
+            k = filtered_token(k_tap, tap_table, tap_row, 0, k_0, k_1, k_2)
+            v = filtered_token(v_tap, tap_table, tap_row, 1, v_0, v_1, v_2)
+            k_1, k_2, v_1, v_2 = k_0, k_1, v_0, v_1
+            x = k * v
             sums = [direct * x, None, None, None]
             for p in range(poles):
                 states[p] = table[pl.ds(bank + p * 8, 8), :] * states[p] + x
                 term = weights[p] * states[p]
                 sums[p % 4] = term if sums[p % 4] is None else sums[p % 4] + term
-            y_ref[0, pl.ds(i * 64 + j, 8, stride=8), :] = (sums[0] + sums[1]) + (sums[2] + sums[3])
-        return tuple(states)
+            y_ref[0, rows, :] = (sums[0] + sums[1]) + (sums[2] + sums[3])
+        return tuple(states) + (k_1, k_2, v_1, v_2)
 
     chunks = block_len // 8
     states = tuple(jnp.zeros((8, LANES), jnp.float32) for _ in range(poles))
+    states += (edges[3], edges[2], edges[5], edges[4])
     states = lax.fori_loop(0, chunks // 2, chunk, states)
     for k in range(0, rounds, 2):
         piece = group - 1 - k // 2
@@ -311,7 +279,7 @@
 def finish_kernel(
     lengths_ref, q_ref, edge_ref, filter_ref, rate_ref, weight_ref, in_ref, y_in, unembed_ref,
     gated_ref, logits_ref,
-    ext_q, y, total,
+    raw_q, turn, tap_table, gated, total,
 ):
     block_len = q_ref.shape[1]
     poles = rate_ref.shape[0] // 8
@@ -321,62 +289,51 @@
     cut = jnp.int32(block_len)
     for first in firsts:
         cut = jnp.where(first >= first_pos, jnp.minimum(cut, first - first_pos), cut)
-    load_block(ext_q, q_ref)
-    load_edge(ext_q, edge_ref, 0)
+    load_block(raw_q, q_ref)
+    edges = to_sublanes(edge_ref, turn, 8)
+    q_tap = load_taps(filter_ref, turn, 0, tap_table, 0)
     tiles = [pl.ds(p * 8, 8) for p in range(poles)]
     decays = [jnp.exp(-rate_ref[tile, :]) for tile in tiles]
     fading = tuple(weight_ref[tile, :] * in_ref[tile, :] * d for tile, d in zip(tiles, decays))
 
-    def fade_chunk(i, fading):
-        fading = list(fading)
+    def gate_chunk(i, carry, carried):
+        (q_1, q_2), fading = carry[:2], carry[2:]
+        place = first_pos + i * 8
+        after = any_between(firsts, place - 1, place)
         for j in range(8):
-            sums = [fading[0], fading[1], fading[2], fading[3]]
-            for p in range(4, poles):
-                sums[p % 4] = sums[p % 4] + fading[p]
-            arrived = (sums[0] + sums[1]) + (sums[2] + sums[3])
             rows = pl.ds(i * 64 + j, 8, stride=8)
-            y[rows, :] = jnp.where(i * 8 + j < cut, 1.0, 0.0) * arrived
-            fading = [f * d for f, d in zip(fading, decays)]
-        return tuple(fading)
+            starts = any_between(firsts, place + j, place + j + 1)
+            tap_row = jnp.where(starts, 16, jnp.where(after, 32, 0))
+            after = starts
+            q_0 = raw_q[rows, :]
+            q = filtered_token(q_tap, tap_table, tap_row, 0, q_0, q_1, q_2)
+            q_1, q_2 = q_0, q_1
+            y = y_in[0, rows, :]
+            if carried:
+                sums = list(fading[:4])
+                for p in range(4, poles):
+                    sums[p % 4] = sums[p % 4] + fading[p]
+                arrived = (sums[0] + sums[1]) + (sums[2] + sums[3])
+                y = y + jnp.where(i * 8 + j < cut, 1.0, 0.0) * arrived
+                fading = [f * d for f, d in zip(fading, decays)]
+            gated[rows, :] = q * y
+        return (q_1, q_2) + tuple(fading)
 
     carried = (cut + 7) // 8
-    lax.fori_loop(0, carried, fade_chunk, fading)
-
-    def plain_chunk(i, _):
-        rows = pl.ds(pl.multiple_of(i * 64, 64), 64)
-        y[rows, :] = jnp.zeros((64, LANES), jnp.float32)
+    carry = (edges[1], edges[0]) + fading
+    carry = lax.fori_loop(0, carried, functools.partial(gate_chunk, carried=True), carry)
+    lax.fori_loop(carried, block_len // 8, functools.partial(gate_chunk, carried=False), carry[:2])
+
+    def round_step(i, _):
+        for ct in range(8):
+            halves = [
+                gated[pl.ds(pl.multiple_of(i * 128 + side * 64 + ct * 8, 8), 8), :] for side in range(2)
+            ]
+            both = jnp.concatenate(halves, axis=0).astype(jnp.bfloat16)
+            gated_ref[pl.ds(pl.multiple_of(i * 16, 16), 16), pl.ds(ct * LANES, LANES)] = both
         return 0
 
-    lax.fori_loop(carried, block_len // 8, plain_chunk, 0)
-
-    def gate(i, ct, taps, masks):
-        halves = []
-        for side in range(2):
-            tile = i * 2 + side
-            q = filter_tile(ext_q, taps, tile, ct, masks[side])
-            rows = pl.ds(pl.multiple_of(tile * 64 + ct * 8, 8), 8)
-            halves.append(q * (y_in[0, rows, :] + y[rows, :]))
-        both = jnp.concatenate(halves, axis=0).astype(jnp.bfloat16)
-        gated_ref[pl.ds(pl.multiple_of(i * 16, 16), 16), pl.ds(ct * LANES, LANES)] = both
-
-    for ct in range(8):
-        taps = load_taps(filter_ref, 0, ct)
-
-        def gate_step(i, _):
-            gate(i, ct, taps, [None, None])
-            return 0
-
-        lax.fori_loop(0, block_len // 16, gate_step, 0, unroll=4)
-
-    def regate(i):
-        masks = []
-        for side in range(2):
-            pair = tile_masks(firsts, first_pos + i * 16 + side * 8)
-            masks.append([jnp.where(m, 1.0, 0.0) for m in pair])
-        for ct in range(8):
-            gate(i, ct, load_taps(filter_ref, 0, ct), masks)
-
-    at_starts(firsts, first_pos, block_len, 16, regate)
+    lax.fori_loop(0, block_len // 16, round_step, 0, unroll=2)
     part = jnp.dot(gated_ref[...], unembed_ref[...], preferred_element_type=jnp.float32)
 
     @pl.when(group == 0)
@@ -472,13 +429,11 @@
         ],
         out_specs=[y_spec, pl.BlockSpec((8, chans), lambda g: (0, 0)), rows_spec, rows_spec, rows_spec],
         scratch_shapes=[
-            pltpu.VMEM((8 * (block_len + 8), LANES), f32),
-            pltpu.VMEM((8 * (block_len + 8), LANES), f32),
+            pltpu.VMEM((block_len * 8, LANES), f32),
+            pltpu.VMEM((block_len * 8, LANES), f32),
             pltpu.VMEM((poles * 8, LANES), f32),
-            pltpu.VMEM((block_len * 8, LANES), f32),
-            pltpu.VMEM((block_len, LANES), f32),
-            pltpu.VMEM((block_len, LANES), f32),
             pltpu.VMEM((2 * poles * 8, LANES), f32),
+            pltpu.VMEM((96, LANES), f32),
             pltpu.VMEM((rows, LANES), f32),
             pltpu.VMEM((16, chans // 2), bf16),
             pltpu.VMEM((16, chans // 2), bf16),
@@ -508,7 +463,9 @@
             pl.BlockSpec((block_len, vocab), lambda g: (0, 0)),
         ],
         scratch_shapes=[
-            pltpu.VMEM((8 * (block_len + 8), LANES), f32),
+            pltpu.VMEM((block_len * 8, LANES), f32),
+            pltpu.VMEM((64, LANES), f32),
+            pltpu.VMEM((48, LANES), f32),
             pltpu.VMEM((block_len * 8, LANES), f32),
             pltpu.VMEM((block_len, vocab), f32),
         ],

time: 56.4 us -> 57.1 us (1.012)
  Pallas kernels: 50.6 us -> 55.1 us
  local copies, waits for them, and re-layouts: 4.76 us -> 1.22 us
    unnamed x13 -> x1, local copies, waits for them, and re-layouts: 4.76 us -> 1.22 us
    pallas_call x1, Pallas kernels: 12.3 us -> 15.1 us  [local(): pl.pallas_call(finish_kernel, name='finish', grid=(groups,), out_shape=[s...]
    pallas_call x1, Pallas kernels: 6.9 us -> 8.49 us  [local(): pl.pallas_call(functools.partial(loss_kernel, parts), name='loss', out_sh...]
where the time goes in v4:
time: 57.1 us; the launch traced here: 56.9 us
  Pallas kernels  55.1 us (96%)
  local copies, waits for them, and re-layouts  1.22 us (2%)
  between operations  0.65 us (1%)
    pallas_call x1, Pallas kernels, local(): pl.pallas_call(functools.partial(recur_kernel, blocks, groups), name='rec...  31.4 us
    pallas_call x1, Pallas kernels, local(): pl.pallas_call(finish_kernel, name='finish', grid=(groups,), out_shape=[s...  15.1 us
    pallas_call x1, Pallas kernels, local(): pl.pallas_call(functools.partial(loss_kernel, parts), name='loss', out_sh...  8.49 us
    unnamed x1, local copies, waits for them, and re-layouts  1.22 us

profile of v4, /device:TPU:29, one launch (start us, length us, event | category | flops | bytes accessed | tf_op | source)
XLA Modules:
  0.0 56.9 jit_solution(5159081694919968614)
XLA Ops:
  0.6 31.4 %recur.1 = (f32[4,2048,128]{2,1,0:T(8,128)}, f32[8,4096]{1,0:T(8,128)}, f32[512,128]{1,0:T(8,128)}, f32[512,128]{1,0:T(8,128)}, f32[512,128]{1,0:T(8,128)}) custom-call(s32[4]{0:T(128)} %lengths_ref.3, bf16[3,256,4096]{2,1,0:T(8,128)(2,1)} %q_ref.1, bf16[3,256,4096]{2,1,0:T(8,128)(2,1)} %q_ref.1, bf16[3,256,4096]{2,1,0:T(8,128)(2,1)} %q_ref.1, ...), custom_call_target="tpu_custom_call" | custom-call | tf_op jit(solution)/shard_map/recur/pallas_call | solution.py:413
  32.1 15.1 %finish.1 = (bf16[256,4096]{1,0:T(8,128)(2,1)}, bf16[256,512]{1,0:T(8,128)(2,1)}) custom-call(s32[4]{0:T(128)} %lengths_ref.3, bf16[3,256,4096]{2,1,0:T(8,128)(2,1)} %q_ref.1, f32[8,4096]{1,0:T(8,128)} %get-tuple-element.9.edge_ref, f32[3,3,4096]{2,1,0:T(4,128)} %filter_ref.3, f32[512,128]{1,0:T(8,128)} %get-tuple-element.10.rate_ref, ...), custom_call_target="tpu_custom_call" | custom-call | tf_op jit(solution)/shard_map/finish/pallas_call | solution.py:452
  47.2 8.5 %loss.1 = f32[2,128]{1,0:T(2,128)} custom-call(bf16[256,512]{1,0:T(8,128)(2,1)} %get-tuple-element.15.logits_ref, s32[2,128]{1,0:T(2,128)} %bitcast.5), custom_call_target="tpu_custom_call" | custom-call | tf_op jit(solution)/shard_map/loss/pallas_call | solution.py:478
  55.7 1.2 %copy.11 = f32[256]{0:T(256)} copy(f32[256]{0:T(256)} %bitcast.4) | data formatting | bytes 2048

commit v5 on v3

--- a/solution.py
+++ b/solution.py
@@ -10,7 +10,8 @@
 MESH = pl.DeviceIdType.MESH
 LANES = 128
 GROUP = 8 * LANES
-VMEM_LIMIT = 48 * 1024 * 1024
+VMEM_LIMIT = 40 * 1024 * 1024
+RECUR_VMEM_LIMIT = 56 * 1024 * 1024
 
 
 def doc_firsts(lengths_ref):
@@ -97,18 +98,40 @@
     return [pos - shift >= start for shift in (1, 2)]
 
 
-def to_sublanes(ref, scratch, row_count):
+def load_tiles(raw, stream_ref):
+    block_len = stream_ref.shape[1]
+
+    def step(i, _):
+        rows = pl.ds(pl.multiple_of(i * 16, 16), 16)
+        for ct in range(8):
+            tile = stream_ref[0, rows, pl.ds(ct * LANES, LANES)].astype(jnp.float32)
+            raw[pl.ds(pl.multiple_of(i * 128 + ct * 8, 8), 8), :] = tile[0:8]
+            raw[pl.ds(pl.multiple_of(i * 128 + 64 + ct * 8, 8), 8), :] = tile[8:16]
+        return 0
+
+    lax.fori_loop(0, block_len // 16, step, 0, unroll=2)
+
+
+def turned_taps(filter_ref, turn, stream_id, first_col):
+    for ct in range(8):
+        turn[pl.ds(ct * 8, 3), :] = filter_ref[stream_id, :, pl.ds(first_col + ct * LANES, LANES)]
+    return [turn[pl.ds(shift, 8, stride=8), :] for shift in range(3)]
+
+
+def to_sublanes(ref, scratch, row_count, first_col=0):
     for top in range(0, row_count, 8):
         for ct in range(8):
-            scratch[pl.ds(top * 8 + ct * 8, 8), :] = ref[top : top + 8, pl.ds(ct * LANES, LANES)]
+            scratch[pl.ds(top * 8 + ct * 8, 8), :] = ref[
+                top : top + 8, pl.ds(first_col + ct * LANES, LANES)
+            ]
     return [scratch[pl.ds((p // 8) * 64 + p % 8, 8, stride=8), :] for p in range(row_count)]
 
 
 def recur_kernel(
     blocks, groups,
-    lengths_ref, tail_ref, k_ref, v_ref, filter_ref, rate_ref, residue_ref, direct_ref,
+    lengths_ref, tail_ref, k_ref, v_ref, filter_hbm, rate_hbm, residue_hbm, direct_hbm,
     y_ref, edge_ref, rate_out, weight_out, in_ref,
-    ext_k, ext_v, turn, driver, mask_1, mask_2, table, ends,
+    raw_k, raw_v, turn, keeps, ends, filter_ref, rate_ref, residue_ref, direct_ref, fetch_sem,
     packed, landed, outbox, inbox, edge_send, edge_recv, send_sem, recv_sem,
 ):
     block_len = k_ref.shape[1]
@@ -180,8 +203,22 @@
         if k + 1 < rounds:
             send(k + 1, piece)
 
+    fetches = [
+        pltpu.make_async_copy(src, dst, fetch_sem.at[n])
+        for n, (src, dst) in enumerate(
+            (
+                (filter_hbm, filter_ref),
+                (rate_hbm, rate_ref),
+                (residue_hbm, residue_ref),
+                (direct_hbm, direct_ref),
+            )
+        )
+    ]
+
     @pl.when(group == 0)
     def _():
+        for fetch in fetches:
+            fetch.start()
         rows = []
         for side in range(2):
             cols = pl.ds(side * half, half)
@@ -200,27 +237,36 @@
             edge_copy.start()
 
         in_ref[...] = jnp.zeros_like(in_ref)
-        table[pl.ds(span, span), :] = jnp.zeros((span, LANES), jnp.float32)
-        for i in range(block_len // 8):
-            masks = tile_masks(firsts, first_pos + i * 8)
-            mask_1[pl.ds(i * 8, 8), :] = jnp.where(masks[0], 1.0, 0.0)
-            mask_2[pl.ds(i * 8, 8), :] = jnp.where(masks[1], 1.0, 0.0)
-
-    load_block(ext_k, k_ref)
-    load_block(ext_v, v_ref)
-
-    rates = to_sublanes(rate_ref, turn, poles)
+
+        def keep_step(i, _):
+            place = first_pos + i * 8 + lax.broadcasted_iota(jnp.int32, (64, LANES), 0) // 8
+            keep = jnp.ones((64, LANES), jnp.float32)
+            for first in firsts:
+                keep = jnp.where(place == first, 0.0, keep)
+            keeps[pl.ds(pl.multiple_of(i * 64, 64), 64), :] = keep
+            return 0
+
+        lax.fori_loop(0, block_len // 8, keep_step, 0)
+        for fetch in fetches:
+            fetch.wait()
+
+    load_tiles(raw_k, k_ref)
+    load_tiles(raw_v, v_ref)
+    first_col = pl.multiple_of(group * GROUP, GROUP)
+
+    rates = to_sublanes(rate_ref, turn, poles, first_col)
     decays = [jnp.exp(-r) for r in rates]
     own = pl.multiple_of(group * span, span)
     for p in range(poles):
         rate_out[pl.ds(own + p * 8, 8), :] = rates[p]
-        table[pl.ds(p * 8, 8), :] = decays[p]
-    residues = to_sublanes(residue_ref, turn, poles)
+    residues = to_sublanes(residue_ref, turn, poles, first_col)
     weights = [residues[p] * (1.0 - decays[p]) for p in range(poles)]
     for p in range(poles):
         weight_out[pl.ds(own + p * 8, 8), :] = weights[p]
     for ct in range(8):
-        turn[pl.ds(ct * 8, 8), :] = jnp.broadcast_to(direct_ref[:, pl.ds(ct * LANES, LANES)], (8, LANES))
+        turn[pl.ds(ct * 8, 8), :] = jnp.broadcast_to(
+            direct_ref[:, pl.ds(first_col + ct * LANES, LANES)], (8, LANES)
+        )
     direct = turn[pl.ds(0, 8, stride=8), :]
 
     @pl.when(group == 0)
@@ -236,40 +282,32 @@
         def _():
             edge_ref[...] = jnp.zeros_like(edge_ref)
 
-    first_col = pl.multiple_of(group * GROUP, GROUP)
-    load_edge(ext_k, edge_ref, 1, first_col)
-    load_edge(ext_v, edge_ref, 2, first_col)
-
-    for ct in range(8):
-        k_taps = load_taps(filter_ref, 1, ct)
-        v_taps = load_taps(filter_ref, 2, ct)
-
-        def filter_step(i, _):
-            rows = pl.ds(pl.multiple_of(i * 8, 8), 8)
-            masks = (mask_1[rows, :], mask_2[rows, :])
-            k = filter_tile(ext_k, k_taps, i, ct, masks)
-            v = filter_tile(ext_v, v_taps, i, ct, masks)
-            driver[pl.ds(pl.multiple_of(i * 64 + ct * 8, 8), 8), :] = k * v
-            return 0
-
-        lax.fori_loop(0, block_len // 8, filter_step, 0, unroll=8)
-
-    def chunk(i, states):
-        states = list(states)
+    edges = to_sublanes(edge_ref, turn, 8, first_col)
+    k_taps = turned_taps(filter_ref, turn, 1, first_col)
+    v_taps = turned_taps(filter_ref, turn, 2, first_col)
+
+    def chunk(i, carry):
+        states, (k_1, k_2, v_1, v_2) = list(carry[:poles]), carry[poles:]
         for j in range(8):
-            x = driver[pl.ds(i * 64 + j, 8, stride=8), :]
-            place = first_pos + i * 8 + j
-            bank = jnp.where(any_between(firsts, place, place + 1), span, 0)
+            rows = pl.ds(i * 64 + j, 8, stride=8)
+            keep = keeps[pl.ds(pl.multiple_of(i * 64 + j * 8, 8), 8), :]
+            k_0, v_0 = raw_k[rows, :], raw_v[rows, :]
+            k_1, k_2, v_1, v_2 = k_1 * keep, k_2 * keep, v_1 * keep, v_2 * keep
+            k = k_taps[0] * k_0 + k_taps[1] * k_1 + k_taps[2] * k_2
+            v = v_taps[0] * v_0 + v_taps[1] * v_1 + v_taps[2] * v_2
+            k_1, k_2, v_1, v_2 = k_0, k_1, v_0, v_1
+            x = k * v
             sums = [direct * x, None, None, None]
             for p in range(poles):
-                states[p] = table[pl.ds(bank + p * 8, 8), :] * states[p] + x
+                states[p] = (decays[p] * keep) * states[p] + x
                 term = weights[p] * states[p]
                 sums[p % 4] = term if sums[p % 4] is None else sums[p % 4] + term
-            y_ref[0, pl.ds(i * 64 + j, 8, stride=8), :] = (sums[0] + sums[1]) + (sums[2] + sums[3])
-        return tuple(states)
+            y_ref[0, rows, :] = (sums[0] + sums[1]) + (sums[2] + sums[3])
+        return tuple(states) + (k_1, k_2, v_1, v_2)
 
     chunks = block_len // 8
     states = tuple(jnp.zeros((8, LANES), jnp.float32) for _ in range(poles))
+    states += (edges[3], edges[2], edges[5], edges[4])
     states = lax.fori_loop(0, chunks // 2, chunk, states)
     for k in range(0, rounds, 2):
         piece = group - 1 - k // 2
@@ -440,8 +478,9 @@
     f32, bf16 = jnp.float32, jnp.bfloat16
     shape = jax.ShapeDtypeStruct
     vmem = pl.BlockSpec(memory_space=pltpu.VMEM)
+    hbm = pl.BlockSpec(memory_space=pltpu.HBM)
     smem = pl.BlockSpec(memory_space=pltpu.SMEM)
-    params = functools.partial(pltpu.CompilerParams, vmem_limit_bytes=VMEM_LIMIT)
+    params = functools.partial(pltpu.CompilerParams, has_side_effects=True)
 
     def stream_spec(j):
         return pl.BlockSpec((1, block_len, GROUP), lambda g: (j, 0, g))
@@ -449,7 +488,6 @@
     rounds = max(1, (blocks - 1).bit_length())
     rows = poles * groups * 8
     filter_spec = pl.BlockSpec((3, 3, GROUP), lambda g: (0, 0, g))
-    pole_spec = pl.BlockSpec((poles, GROUP), lambda g: (0, g))
     rows_spec = pl.BlockSpec((rows, LANES), lambda g: (0, 0))
     y_spec = pl.BlockSpec((1, block_len * 8, LANES), lambda g: (g, 0, 0))
 
@@ -467,19 +505,20 @@
         in_specs=[
             smem,
             pl.BlockSpec((3, 16, chans), lambda g: (0, block_len // 16 - 1, 0)),
-            stream_spec(1), stream_spec(2), filter_spec, pole_spec, pole_spec,
-            pl.BlockSpec((1, GROUP), lambda g: (0, g)),
+            stream_spec(1), stream_spec(2), hbm, hbm, hbm, hbm,
         ],
         out_specs=[y_spec, pl.BlockSpec((8, chans), lambda g: (0, 0)), rows_spec, rows_spec, rows_spec],
         scratch_shapes=[
-            pltpu.VMEM((8 * (block_len + 8), LANES), f32),
-            pltpu.VMEM((8 * (block_len + 8), LANES), f32),
+            pltpu.VMEM((block_len * 8, LANES), f32),
+            pltpu.VMEM((block_len * 8, LANES), f32),
             pltpu.VMEM((poles * 8, LANES), f32),
             pltpu.VMEM((block_len * 8, LANES), f32),
-            pltpu.VMEM((block_len, LANES), f32),
-            pltpu.VMEM((block_len, LANES), f32),
-            pltpu.VMEM((2 * poles * 8, LANES), f32),
             pltpu.VMEM((rows, LANES), f32),
+            pltpu.VMEM((3, 3, chans), f32),
+            pltpu.VMEM((poles, chans), f32),
+            pltpu.VMEM((poles, chans), f32),
+            pltpu.VMEM((1, chans), f32),
+            pltpu.SemaphoreType.DMA((4,)),
             pltpu.VMEM((16, chans // 2), bf16),
             pltpu.VMEM((16, chans // 2), bf16),
             pltpu.VMEM((rounds, rows, LANES), bf16),
@@ -489,7 +528,7 @@
             pltpu.SemaphoreType.DMA((rounds, groups)),
             pltpu.SemaphoreType.DMA((rounds, groups)),
         ],
-        compiler_params=params(collective_id=0, has_side_effects=True),
+        compiler_params=params(collective_id=0, vmem_limit_bytes=RECUR_VMEM_LIMIT),
     )(doc_lengths, streams, streams, streams, short_filter, pole_rates, residues, direct.reshape(1, chans))
 
     turned_spec = pl.BlockSpec((poles * 8, LANES), lambda g: (g, 0))
@@ -512,7 +551,7 @@
             pltpu.VMEM((block_len * 8, LANES), f32),
             pltpu.VMEM((block_len, vocab), f32),
         ],
-        compiler_params=params(),
+        compiler_params=pltpu.CompilerParams(vmem_limit_bytes=VMEM_LIMIT),
     )(
         doc_lengths, streams, edges, short_filter, rates, weights,
         incoming, y_local, unembed,
@@ -529,7 +568,7 @@
             pltpu.SemaphoreType.DMA((max(1, parts - 1),)),
             pltpu.SemaphoreType.DMA((max(1, parts - 1),)),
         ],
-        compiler_params=params(collective_id=1, has_side_effects=True),
+        compiler_params=params(collective_id=1, vmem_limit_bytes=VMEM_LIMIT),
     )(logits, targets.reshape(block_len // LANES, LANES))
     return gated_out, loss.reshape(block_len)
 

time: 56.4 us -> 58.6 us (1.039)
  local copies, waits for them, and re-layouts: 4.76 us -> 6.51 us
    unnamed x13 -> x19, local copies, waits for them, and re-layouts: 4.76 us -> 6.51 us
    pallas_call x1, Pallas kernels: 31.4 us -> 32.6 us  [local(): pl.pallas_call(functools.partial(recur_kernel, blocks, groups), name='rec...]
where the time goes in v5:
time: 58.6 us; the launch traced here: 58.3 us
  Pallas kernels  51 us (87%)
  local copies, waits for them, and re-layouts  6.51 us (11%)
  between operations  0.71 us (1%)
    pallas_call x1, Pallas kernels, local(): pl.pallas_call(functools.partial(recur_kernel, blocks, groups), name='rec...  32.6 us
    pallas_call x1, Pallas kernels, local(): pl.pallas_call(finish_kernel, name='finish', grid=(groups,), out_shape=[s...  11.9 us
    pallas_call x1, Pallas kernels, local(): pl.pallas_call(functools.partial(loss_kernel, parts), name='loss', out_sh...  6.53 us
    unnamed x19, local copies, waits for them, and re-layouts  6.51 us

profile of v5, /device:TPU:29, one launch (start us, length us, event | category | flops | bytes accessed | tf_op | source)
XLA Modules:
  0.0 58.3 jit_solution(11032491163704589289)
XLA Ops:
  0.6 0.0 copy-start
  0.6 0.0 copy-start.2
  0.7 0.0 copy-start.7
  0.7 32.6 %recur.1 = (f32[4,2048,128]{2,1,0:T(8,128)}, f32[8,4096]{1,0:T(8,128)}, f32[512,128]{1,0:T(8,128)}, f32[512,128]{1,0:T(8,128)}, f32[512,128]{1,0:T(8,128)}) custom-call(s32[4]{0:T(128)} %lengths_ref.3, bf16[3,256,4096]{2,1,0:T(8,128)(2,1)} %q_ref.1, bf16[3,256,4096]{2,1,0:T(8,128)(2,1)} %q_ref.1, bf16[3,256,4096]{2,1,0:T(8,128)(2,1)} %q_ref.1, ...), custom_call_target="tpu_custom_call" | custom-call | tf_op jit(solution)/shard_map/recur/pallas_call | solution.py:494
  33.3 0.0 copy-done
  33.3 0.0 copy-done.2
  33.3 0.0 copy-done.7
  33.3 0.0 copy-start.1
  33.3 2.2 %copy-done.1 = f32[4,2048,128]{2,1,0:T(8,128)S(1)} copy-done((f32[4,2048,128]{2,1,0:T(8,128)S(1)}, f32[4,2048,128]{2,1,0:T(8,128)}, u32[]{:S(2)}) %copy-start.1) | copy-done | bytes 4194328
  35.5 0.0 copy-start.3
  35.5 0.9 %copy-done.3 = f32[512,128]{1,0:T(8,128)S(1)} copy-done((f32[512,128]{1,0:T(8,128)S(1)}, f32[512,128]{1,0:T(8,128)}, u32[]{:S(2)}) %copy-start.3) | copy-done | bytes 262168
  36.5 0.0 copy-start.4
  36.5 0.9 %copy-done.4 = f32[512,128]{1,0:T(8,128)S(1)} copy-done((f32[512,128]{1,0:T(8,128)S(1)}, f32[512,128]{1,0:T(8,128)}, u32[]{:S(2)}) %copy-start.4) | copy-done | bytes 262168
  37.4 0.0 copy-start.5
  37.4 0.9 %copy-done.5 = f32[512,128]{1,0:T(8,128)S(1)} copy-done((f32[512,128]{1,0:T(8,128)S(1)}, f32[512,128]{1,0:T(8,128)}, u32[]{:S(2)}) %copy-start.5) | copy-done | bytes 262168
  38.4 0.0 copy-start.6
  38.4 0.9 %copy-done.6 = f32[8,4096]{1,0:T(8,128)S(1)} copy-done((f32[8,4096]{1,0:T(8,128)S(1)}, f32[8,4096]{1,0:T(8,128)}, u32[]{:S(2)}) %copy-start.6) | copy-done | bytes 131096
  39.3 0.0 copy-start.8
  39.3 11.9 %finish.1 = (bf16[256,4096]{1,0:T(8,128)(2,1)}, bf16[256,512]{1,0:T(8,128)(2,1)S(1)}) custom-call(s32[4]{0:T(128)S(1)} %copy-done.7, bf16[3,256,4096]{2,1,0:T(8,128)(2,1)} %q_ref.1, f32[8,4096]{1,0:T(8,128)S(1)} %copy-done.6, f32[3,3,4096]{2,1,0:T(4,128)S(1)} %copy-done.2, f32[512,128]{1,0:T(8,128)S(1)} %copy-done.3, f32[512,128]{1,0:T(8,128)S(1)} %copy-done.4, ...), custom_call_target="tpu_custom_call" | custom-call | tf_op jit(solution)/shard_map/finish/pallas_call | solution.py:536
  51.1 0.0 copy-done.8
  51.1 6.5 %loss.1 = f32[2,128]{1,0:T(2,128)S(1)} custom-call(bf16[256,512]{1,0:T(8,128)(2,1)S(1)} %get-tuple-element.15.logits_ref, s32[2,128]{1,0:T(2,128)S(1)} %bitcast.4), custom_call_target="tpu_custom_call" | custom-call | tf_op jit(solution)/shard_map/loss/pallas_call | solution.py:560
  57.7 0.6 copy.11
Async XLA Ops:
  0.6 32.7 %copy-start = (bf16[4096,512]{1,0:T(8,128)(2,1)S(1)}, bf16[4096,512]{1,0:T(8,128)(2,1)}, u32[]{:S(2)}) copy-start(bf16[4096,512]{1,0:T(8,128)(2,1)} %unembed_ref.1) | copy-start | bytes 12582916
  0.6 32.7 %copy-start.2 = (f32[3,3,4096]{2,1,0:T(4,128)S(1)}, f32[3,3,4096]{2,1,0:T(4,128)}, u32[]{:S(2)}) copy-start(f32[3,3,4096]{2,1,0:T(4,128)} %filter_ref.1) | copy-start | bytes 442372
  0.7 32.7 %copy-start.7 = (s32[4]{0:T(128)S(1)}, s32[4]{0:T(128)}, u32[]{:S(2)}) copy-start(s32[4]{0:T(128)} %lengths_ref.3) | copy-start | bytes 52
  33.3 2.2 %copy-start.1 = (f32[4,2048,128]{2,1,0:T(8,128)S(1)}, f32[4,2048,128]{2,1,0:T(8,128)}, u32[]{:S(2)}) copy-start(f32[4,2048,128]{2,1,0:T(8,128)} %get-tuple-element.13.y_in) | copy-start | bytes 12582916
  35.5 0.9 %copy-start.3 = (f32[512,128]{1,0:T(8,128)S(1)}, f32[512,128]{1,0:T(8,128)}, u32[]{:S(2)}) copy-start(f32[512,128]{1,0:T(8,128)} %get-tuple-element.10.rate_ref) | copy-start | bytes 786436
  36.5 0.9 %copy-start.4 = (f32[512,128]{1,0:T(8,128)S(1)}, f32[512,128]{1,0:T(8,128)}, u32[]{:S(2)}) copy-start(f32[512,128]{1,0:T(8,128)} %get-tuple-element.11.weight_ref) | copy-start | bytes 786436
  37.4 0.9 %copy-start.5 = (f32[512,128]{1,0:T(8,128)S(1)}, f32[512,128]{1,0:T(8,128)}, u32[]{:S(2)}) copy-start(f32[512,128]{1,0:T(8,128)} %get-tuple-element.12.in_ref) | copy-start | bytes 786436
  38.4 0.9 %copy-start.6 = (f32[8,4096]{1,0:T(8,128)S(1)}, f32[8,4096]{1,0:T(8,128)}, u32[]{:S(2)}) copy-start(f32[8,4096]{1,0:T(8,128)} %get-tuple-element.9.edge_ref) | copy-start | bytes 393220
  39.3 11.9 %copy-start.8 = (s32[256]{0:T(256)S(1)}, s32[256]{0:T(256)}, u32[]{:S(2)}) copy-start(s32[256]{0:T(256)} %param.14) | copy-start | bytes 3076

commit v6 on v3

--- a/solution.py
+++ b/solution.py
@@ -10,7 +10,8 @@
 MESH = pl.DeviceIdType.MESH
 LANES = 128
 GROUP = 8 * LANES
-VMEM_LIMIT = 48 * 1024 * 1024
+VMEM_LIMIT = 65200 * 1024
+LOSS_VMEM_LIMIT = 40 * 1024 * 1024
 
 
 def doc_firsts(lengths_ref):
@@ -97,10 +98,44 @@
     return [pos - shift >= start for shift in (1, 2)]
 
 
-def to_sublanes(ref, scratch, row_count):
+def load_tiles(raw, stream_ref):
+    block_len = stream_ref.shape[1]
+
+    def step(i, _):
+        rows = pl.ds(pl.multiple_of(i * 16, 16), 16)
+        for ct in range(8):
+            tile = stream_ref[0, rows, pl.ds(ct * LANES, LANES)].astype(jnp.float32)
+            raw[pl.ds(pl.multiple_of(i * 128 + ct * 8, 8), 8), :] = tile[0:8]
+            raw[pl.ds(pl.multiple_of(i * 128 + 64 + ct * 8, 8), 8), :] = tile[8:16]
+        return 0
+
+    lax.fori_loop(0, block_len // 16, step, 0, unroll=2)
+
+
+def bank_taps(filter_ref, turn, stream_id, bank_table, slot):
+    for ct in range(8):
+        turn[pl.ds(ct * 8, 3), :] = filter_ref[stream_id, :, pl.ds(ct * LANES, LANES)]
+    taps = [turn[pl.ds(shift, 8, stride=8), :] for shift in range(3)]
+    width = bank_table.shape[0] // 3
+    zero = jnp.zeros((8, LANES), jnp.float32)
+    for bank, pair in enumerate(((taps[1], taps[2]), (zero, zero), (taps[1], zero))):
+        for n in range(2):
+            bank_table[pl.ds(bank * width + (slot * 2 + n) * 8, 8), :] = pair[n]
+    return taps[0]
+
+
+def filtered_token(tap, bank_table, bank_row, slot, now, back_1, back_2):
+    tap_1 = bank_table[pl.ds(bank_row + slot * 16, 8), :]
+    tap_2 = bank_table[pl.ds(bank_row + slot * 16 + 8, 8), :]
+    return tap * now + tap_1 * back_1 + tap_2 * back_2
+
+
+def to_sublanes(ref, scratch, row_count, first_col=0):
     for top in range(0, row_count, 8):
         for ct in range(8):
-            scratch[pl.ds(top * 8 + ct * 8, 8), :] = ref[top : top + 8, pl.ds(ct * LANES, LANES)]
+            scratch[pl.ds(top * 8 + ct * 8, 8), :] = ref[
+                top : top + 8, pl.ds(first_col + ct * LANES, LANES)
+            ]
     return [scratch[pl.ds((p // 8) * 64 + p % 8, 8, stride=8), :] for p in range(row_count)]
 
 
@@ -108,7 +143,7 @@
     blocks, groups,
     lengths_ref, tail_ref, k_ref, v_ref, filter_ref, rate_ref, residue_ref, direct_ref,
     y_ref, edge_ref, rate_out, weight_out, in_ref,
-    ext_k, ext_v, turn, driver, mask_1, mask_2, table, ends,
+    raw_k, raw_v, turn, table, tap_table, ends,
     packed, landed, outbox, inbox, edge_send, edge_recv, send_sem, recv_sem,
 ):
     block_len = k_ref.shape[1]
@@ -201,13 +236,9 @@
 
         in_ref[...] = jnp.zeros_like(in_ref)
         table[pl.ds(span, span), :] = jnp.zeros((span, LANES), jnp.float32)
-        for i in range(block_len // 8):
-            masks = tile_masks(firsts, first_pos + i * 8)
-            mask_1[pl.ds(i * 8, 8), :] = jnp.where(masks[0], 1.0, 0.0)
-            mask_2[pl.ds(i * 8, 8), :] = jnp.where(masks[1], 1.0, 0.0)
-
-    load_block(ext_k, k_ref)
-    load_block(ext_v, v_ref)
+
+    load_tiles(raw_k, k_ref)
+    load_tiles(raw_v, v_ref)
 
     rates = to_sublanes(rate_ref, turn, poles)
     decays = [jnp.exp(-r) for r in rates]
@@ -236,40 +267,36 @@
         def _():
             edge_ref[...] = jnp.zeros_like(edge_ref)
 
-    first_col = pl.multiple_of(group * GROUP, GROUP)
-    load_edge(ext_k, edge_ref, 1, first_col)
-    load_edge(ext_v, edge_ref, 2, first_col)
-
-    for ct in range(8):
-        k_taps = load_taps(filter_ref, 1, ct)
-        v_taps = load_taps(filter_ref, 2, ct)
-
-        def filter_step(i, _):
-            rows = pl.ds(pl.multiple_of(i * 8, 8), 8)
-            masks = (mask_1[rows, :], mask_2[rows, :])
-            k = filter_tile(ext_k, k_taps, i, ct, masks)
-            v = filter_tile(ext_v, v_taps, i, ct, masks)
-            driver[pl.ds(pl.multiple_of(i * 64 + ct * 8, 8), 8), :] = k * v
-            return 0
-
-        lax.fori_loop(0, block_len // 8, filter_step, 0, unroll=8)
-
-    def chunk(i, states):
-        states = list(states)
+    edges = to_sublanes(edge_ref, turn, 8, pl.multiple_of(group * GROUP, GROUP))
+    k_tap = bank_taps(filter_ref, turn, 1, tap_table, 0)
+    v_tap = bank_taps(filter_ref, turn, 2, tap_table, 1)
+
+    def chunk(i, carry):
+        states, (k_1, k_2, v_1, v_2) = list(carry[:poles]), carry[poles:]
+        place = first_pos + i * 8
+        after = any_between(firsts, place - 1, place)
         for j in range(8):
-            x = driver[pl.ds(i * 64 + j, 8, stride=8), :]
-            place = first_pos + i * 8 + j
-            bank = jnp.where(any_between(firsts, place, place + 1), span, 0)
+            rows = pl.ds(i * 64 + j, 8, stride=8)
+            starts = any_between(firsts, place + j, place + j + 1)
+            bank = jnp.where(starts, span, 0)
+            tap_row = jnp.where(starts, 32, jnp.where(after, 64, 0))
+            after = starts
+            k_0, v_0 = raw_k[rows, :], raw_v[rows, :]
+            k = filtered_token(k_tap, tap_table, tap_row, 0, k_0, k_1, k_2)
+            v = filtered_token(v_tap, tap_table, tap_row, 1, v_0, v_1, v_2)
+            k_1, k_2, v_1, v_2 = k_0, k_1, v_0, v_1
+            x = k * v
             sums = [direct * x, None, None, None]
             for p in range(poles):
                 states[p] = table[pl.ds(bank + p * 8, 8), :] * states[p] + x
                 term = weights[p] * states[p]
                 sums[p % 4] = term if sums[p % 4] is None else sums[p % 4] + term
-            y_ref[0, pl.ds(i * 64 + j, 8, stride=8), :] = (sums[0] + sums[1]) + (sums[2] + sums[3])
-        return tuple(states)
+            y_ref[0, rows, :] = (sums[0] + sums[1]) + (sums[2] + sums[3])
+        return tuple(states) + (k_1, k_2, v_1, v_2)
 
     chunks = block_len // 8
     states = tuple(jnp.zeros((8, LANES), jnp.float32) for _ in range(poles))
+    states += (edges[3], edges[2], edges[5], edges[4])
     states = lax.fori_loop(0, chunks // 2, chunk, states)
     for k in range(0, rounds, 2):
         piece = group - 1 - k // 2
@@ -472,13 +499,11 @@
         ],
         out_specs=[y_spec, pl.BlockSpec((8, chans), lambda g: (0, 0)), rows_spec, rows_spec, rows_spec],
         scratch_shapes=[
-            pltpu.VMEM((8 * (block_len + 8), LANES), f32),
-            pltpu.VMEM((8 * (block_len + 8), LANES), f32),
+            pltpu.VMEM((block_len * 8, LANES), f32),
+            pltpu.VMEM((block_len * 8, LANES), f32),
             pltpu.VMEM((poles * 8, LANES), f32),
-            pltpu.VMEM((block_len * 8, LANES), f32),
-            pltpu.VMEM((block_len, LANES), f32),
-            pltpu.VMEM((block_len, LANES), f32),
             pltpu.VMEM((2 * poles * 8, LANES), f32),
+            pltpu.VMEM((96, LANES), f32),
             pltpu.VMEM((rows, LANES), f32),
             pltpu.VMEM((16, chans // 2), bf16),
             pltpu.VMEM((16, chans // 2), bf16),
@@ -529,7 +554,9 @@
             pltpu.SemaphoreType.DMA((max(1, parts - 1),)),
             pltpu.SemaphoreType.DMA((max(1, parts - 1),)),
         ],
-        compiler_params=params(collective_id=1, has_side_effects=True),
+        compiler_params=pltpu.CompilerParams(
+            collective_id=1, has_side_effects=True, vmem_limit_bytes=LOSS_VMEM_LIMIT
+        ),
     )(logits, targets.reshape(block_len // LANES, LANES))
     return gated_out, loss.reshape(block_len)
 

time: 56.4 us -> 53.4 us (0.947)
  the two profiles are of different devices: /device:TPU:29 before, /device:TPU:25 now
where the time goes in v6:
time: 53.4 us; the launch traced here: 53.1 us
  Pallas kernels  50.9 us (95%)
  local copies, waits for them, and re-layouts  1.51 us (3%)
  between operations  0.67 us (1%)
    pallas_call x1, Pallas kernels, local(): pl.pallas_call(functools.partial(recur_kernel, blocks, groups), name='rec...  30.8 us
    pallas_call x1, Pallas kernels, local(): pl.pallas_call(finish_kernel, name='finish', grid=(groups,), out_shape=[s...  12.8 us
    pallas_call x1, Pallas kernels, local(): pl.pallas_call(functools.partial(loss_kernel, parts), name='loss', out_sh...  7.36 us
    unnamed x5, local copies, waits for them, and re-layouts  1.51 us

profile of v6, /device:TPU:25, one launch (start us, length us, event | category | flops | bytes accessed | tf_op | source)
XLA Modules:
  0.0 53.1 jit_solution(2504953974573816817)
XLA Ops:
  0.6 30.8 %recur.1 = (f32[4,2048,128]{2,1,0:T(8,128)}, f32[8,4096]{1,0:T(8,128)}, f32[512,128]{1,0:T(8,128)}, f32[512,128]{1,0:T(8,128)}, f32[512,128]{1,0:T(8,128)}) custom-call(s32[4]{0:T(128)} %lengths_ref.3, bf16[3,256,4096]{2,1,0:T(8,128)(2,1)} %q_ref.1, bf16[3,256,4096]{2,1,0:T(8,128)(2,1)} %q_ref.1, bf16[3,256,4096]{2,1,0:T(8,128)(2,1)} %q_ref.1, ...), custom_call_target="tpu_custom_call" | custom-call | tf_op jit(solution)/shard_map/recur/pallas_call | solution.py:483
  31.5 0.0 copy-start.1
  31.5 12.8 %finish.1 = (bf16[256,4096]{1,0:T(8,128)(2,1)}, bf16[256,512]{1,0:T(8,128)(2,1)}) custom-call(s32[4]{0:T(128)} %lengths_ref.3, bf16[3,256,4096]{2,1,0:T(8,128)(2,1)} %q_ref.1, f32[8,4096]{1,0:T(8,128)} %get-tuple-element.9.edge_ref, f32[3,3,4096]{2,1,0:T(4,128)} %filter_ref.3, f32[512,128]{1,0:T(8,128)} %get-tuple-element.10.rate_ref, ...), custom_call_target="tpu_custom_call" | custom-call | tf_op jit(solution)/shard_map/finish/pallas_call | solution.py:522
  44.2 0.0 copy-done.1
  44.2 0.0 copy-start
  44.3 0.9 %copy-done = bf16[256,512]{1,0:T(8,128)(2,1)S(1)} copy-done((bf16[256,512]{1,0:T(8,128)(2,1)S(1)}, bf16[256,512]{1,0:T(8,128)(2,1)}, u32[]{:S(2)}) %copy-start) | copy-done | bytes 262168
  45.2 7.4 %loss.1 = f32[2,128]{1,0:T(2,128)S(1)} custom-call(bf16[256,512]{1,0:T(8,128)(2,1)S(1)} %copy-done, s32[2,128]{1,0:T(2,128)S(1)} %bitcast.4), custom_call_target="tpu_custom_call" | custom-call | tf_op jit(solution)/shard_map/loss/pallas_call | solution.py:546
  52.6 0.6 %copy.11 = f32[256]{0:T(256)} copy(f32[256]{0:T(256)S(1)} %bitcast.3) | data formatting | bytes 2048
Async XLA Ops:
  31.5 12.8 %copy-start.1 = (s32[256]{0:T(256)S(1)}, s32[256]{0:T(256)}, u32[]{:S(2)}) copy-start(s32[256]{0:T(256)} %param.14) | copy-start | bytes 3076
  44.2 1.0 %copy-start = (bf16[256,512]{1,0:T(8,128)(2,1)S(1)}, bf16[256,512]{1,0:T(8,128)(2,1)}, u32[]{:S(2)}) copy-start(bf16[256,512]{1,0:T(8,128)(2,1)} %get-tuple-element.15.logits_ref) | copy-start | bytes 786436

commit v7 on v6

--- a/solution.py
+++ b/solution.py
@@ -297,7 +297,7 @@
     chunks = block_len // 8
     states = tuple(jnp.zeros((8, LANES), jnp.float32) for _ in range(poles))
     states += (edges[3], edges[2], edges[5], edges[4])
-    states = lax.fori_loop(0, chunks // 2, chunk, states)
+    states = lax.fori_loop(0, chunks // 2, chunk, states, unroll=2)
     for k in range(0, rounds, 2):
         piece = group - 1 - k // 2
 
@@ -305,7 +305,7 @@
         def _():
             relay(k, piece)
 
-    states = lax.fori_loop(chunks // 2, chunks, chunk, states)
+    states = lax.fori_loop(chunks // 2, chunks, chunk, states, unroll=2)
     for p in range(poles):
         ends[pl.ds(own + p * 8, 8), :] = states[p]
     send(0, group)
@@ -356,25 +356,25 @@
 
     def fade_chunk(i, fading):
         fading = list(fading)
-        for j in range(8):
+        for j in range(16):
             sums = [fading[0], fading[1], fading[2], fading[3]]
             for p in range(4, poles):
                 sums[p % 4] = sums[p % 4] + fading[p]
             arrived = (sums[0] + sums[1]) + (sums[2] + sums[3])
-            rows = pl.ds(i * 64 + j, 8, stride=8)
-            y[rows, :] = jnp.where(i * 8 + j < cut, 1.0, 0.0) * arrived
+            rows = pl.ds(i * 128 + j // 8 * 64 + j % 8, 8, stride=8)
+            y[rows, :] = jnp.where(i * 16 + j < cut, 1.0, 0.0) * arrived
             fading = [f * d for f, d in zip(fading, decays)]
         return tuple(fading)
 
-    carried = (cut + 7) // 8
+    carried = (cut + 15) // 16
     lax.fori_loop(0, carried, fade_chunk, fading)
 
     def plain_chunk(i, _):
-        rows = pl.ds(pl.multiple_of(i * 64, 64), 64)
-        y[rows, :] = jnp.zeros((64, LANES), jnp.float32)
+        rows = pl.ds(pl.multiple_of(i * 128, 128), 128)
+        y[rows, :] = jnp.zeros((128, LANES), jnp.float32)
         return 0
 
-    lax.fori_loop(carried, block_len // 8, plain_chunk, 0)
+    lax.fori_loop(carried, block_len // 16, plain_chunk, 0)
 
     def gate(i, ct, taps, masks):
         halves = []

time: 53.4 us -> 53.4 us (level)
  the two profiles are of different devices: /device:TPU:25 before, /device:TPU:29 now
where the time goes in v7:
time: 53.4 us; the launch traced here: 53.2 us
  Pallas kernels  51 us (96%)
  local copies, waits for them, and re-layouts  1.51 us (3%)
  between operations  0.67 us (1%)
    pallas_call x1, Pallas kernels, local(): pl.pallas_call(functools.partial(recur_kernel, blocks, groups), name='rec...  30.3 us
    pallas_call x1, Pallas kernels, local(): pl.pallas_call(finish_kernel, name='finish', grid=(groups,), out_shape=[s...  12.6 us
    pallas_call x1, Pallas kernels, local(): pl.pallas_call(functools.partial(loss_kernel, parts), name='loss', out_sh...  8.1 us
    unnamed x5, local copies, waits for them, and re-layouts  1.51 us

profile of v7, /device:TPU:29, one launch (start us, length us, event | category | flops | bytes accessed | tf_op | source)
XLA Modules:
  0.0 53.2 jit_solution(15859408261505784578)
XLA Ops:
  0.6 30.3 %recur.1 = (f32[4,2048,128]{2,1,0:T(8,128)}, f32[8,4096]{1,0:T(8,128)}, f32[512,128]{1,0:T(8,128)}, f32[512,128]{1,0:T(8,128)}, f32[512,128]{1,0:T(8,128)}) custom-call(s32[4]{0:T(128)} %lengths_ref.3, bf16[3,256,4096]{2,1,0:T(8,128)(2,1)} %q_ref.1, bf16[3,256,4096]{2,1,0:T(8,128)(2,1)} %q_ref.1, bf16[3,256,4096]{2,1,0:T(8,128)(2,1)} %q_ref.1, ...), custom_call_target="tpu_custom_call" | custom-call | tf_op jit(solution)/shard_map/recur/pallas_call | solution.py:483
  30.9 0.0 copy-start.1
  30.9 12.6 %finish.1 = (bf16[256,4096]{1,0:T(8,128)(2,1)}, bf16[256,512]{1,0:T(8,128)(2,1)}) custom-call(s32[4]{0:T(128)} %lengths_ref.3, bf16[3,256,4096]{2,1,0:T(8,128)(2,1)} %q_ref.1, f32[8,4096]{1,0:T(8,128)} %get-tuple-element.9.edge_ref, f32[3,3,4096]{2,1,0:T(4,128)} %filter_ref.3, f32[512,128]{1,0:T(8,128)} %get-tuple-element.10.rate_ref, ...), custom_call_target="tpu_custom_call" | custom-call | tf_op jit(solution)/shard_map/finish/pallas_call | solution.py:522
  43.6 0.0 copy-done.1
  43.6 0.0 copy-start
  43.6 0.9 %copy-done = bf16[256,512]{1,0:T(8,128)(2,1)S(1)} copy-done((bf16[256,512]{1,0:T(8,128)(2,1)S(1)}, bf16[256,512]{1,0:T(8,128)(2,1)}, u32[]{:S(2)}) %copy-start) | copy-done | bytes 262168
  44.5 8.1 %loss.1 = f32[2,128]{1,0:T(2,128)S(1)} custom-call(bf16[256,512]{1,0:T(8,128)(2,1)S(1)} %copy-done, s32[2,128]{1,0:T(2,128)S(1)} %bitcast.4), custom_call_target="tpu_custom_call" | custom-call | tf_op jit(solution)/shard_map/loss/pallas_call | solution.py:546
  52.6 0.6 %copy.11 = f32[256]{0:T(256)} copy(f32[256]{0:T(256)S(1)} %bitcast.3) | data formatting | bytes 2048
Async XLA Ops:
  30.9 12.6 %copy-start.1 = (s32[256]{0:T(256)S(1)}, s32[256]{0:T(256)}, u32[]{:S(2)}) copy-start(s32[256]{0:T(256)} %param.14) | copy-start | bytes 3076
  43.6 1.0 %copy-start = (bf16[256,512]{1,0:T(8,128)(2,1)S(1)}, bf16[256,512]{1,0:T(8,128)(2,1)}, u32[]{:S(2)}) copy-start(bf16[256,512]{1,0:T(8,128)(2,1)} %get-tuple-element.15.logits_ref) | copy-start | bytes 786436
